TPU v7x, 512 devices: a whole 4x4x16 slice. The times are simulated.
512 devices in a mesh: rep: 16 (over x, y), fsdp: 32 (over z, core).
Axes of the slice: x: 4, y: 4, z: 16, core: 2. Of those that a mesh axis runs over, the one named last changes fastest.
Arguments:
- grad_parts: bfloat16 [16, 48, 512, 512], P('rep', None, 'fsdp'), may hold values from -2 to 2
- momentum: float32 [96, 512, 512], P('rep', 'fsdp'), may hold values from -160 to 160
- weight: float32 [48, 512, 512], P(None, 'fsdp'), may hold values from -0.25 to 0.25
- owners: int32 [48], replicated, may hold values from 0 to 15, as said below
Outputs:
- step_update: float32 [48, 512, 512], P(None, 'fsdp')
- new_weight: float32 [48, 512, 512], P(None, 'fsdp')
- new_momentum: float32 [96, 512, 512], P('rep', 'fsdp')
Inputs may be any that keep to these rules, and one draw needn't show every extreme that they name: `owners`: each block names one replica group. No group owns more than 6 blocks, and one group owns exactly 6.
All inputs are finite; a program needn't handle non-finite values.
Results may differ from a plain program's by a relative error of at most 0.025.
Values may be sent and summed in bfloat16 or wider, within the bound.
No kernel may reach another device: no remote copies, remote signals or barrier semaphores. Data moves between devices by JAX's collectives and lax.ppermute only.
A program may use at most 64 MiB of HBM per device.

v0:
```python
import math

import jax
import jax.numpy as jnp
import numpy as np
from jax import lax
from jax.sharding import PartitionSpec as P

NS_ITERS = 3


COEF_A = 3.4445
COEF_B = -4.775
COEF_C = 2.0315
MOMENTUM_DECAY = 0.95
LEARN_RATE = 0.02
EPSILON = 1e-07


def orthogonalize_all(stacked):
    widened = stacked.astype(jnp.float32)
    frobenius = jnp.sqrt(jnp.sum(widened * widened, axis=(1, 2), keepdims=True))
    current = (widened / (frobenius + EPSILON)).astype(jnp.bfloat16)
    for iteration in range(NS_ITERS):
        gram_matrix = jnp.einsum(
            "sij,skj->sik", current, current, preferred_element_type=jnp.float32
        ).astype(jnp.bfloat16)
        square = jnp.einsum(
            "sij,sjk->sik", gram_matrix, gram_matrix, preferred_element_type=jnp.float32
        )
        polynomial = (COEF_B * gram_matrix.astype(jnp.float32) + COEF_C * square).astype(
            jnp.bfloat16
        )
        current = (
            COEF_A * current.astype(jnp.float32)
            + jnp.einsum("sij,sjk->sik", polynomial, current, preferred_element_type=jnp.float32)
        ).astype(jnp.bfloat16)
    return current


def slot_blocks(location, slot_ids):
    count = location.shape[0]
    block_ids = jnp.arange(count, dtype=jnp.int32)
    matching = location[None, :] == slot_ids[:, None]
    present = jnp.sum(matching.astype(jnp.int32), axis=1) > 0
    source = jnp.sum(jnp.where(matching, block_ids[None, :], 0), axis=1)
    return (present, source)


def on_device(grad_parts, momentum, weight, owners):
    local_parts = grad_parts[0]
    block_count = local_parts.shape[0]
    block_order = weight.shape[2]
    members = lax.axis_size("fsdp")
    most_slots = momentum.shape[0]
    job_count = (most_slots + members - 1) // members
    replica_here = lax.axis_index("rep")
    member_here = lax.axis_index("fsdp")
    positions = jnp.arange(block_count, dtype=jnp.int32)
    matching = (owners[None, :] == owners[:, None]) & (positions[None, :] < positions[:, None])
    slot_index = jnp.sum(matching.astype(jnp.int32), axis=1)
    location = owners * most_slots + slot_index
    own_slots = replica_here * most_slots + jnp.arange(most_slots, dtype=jnp.int32)
    occupied, own_source = slot_blocks(location, own_slots)
    occupied = occupied[:, None, None]
    gradient = lax.psum(local_parts.astype(jnp.float32).astype(jnp.bfloat16), "rep").astype(
        jnp.float32
    )
    chosen = jnp.where(occupied, jnp.take(gradient, own_source, axis=0), 0.0)
    advanced = jnp.where(occupied, MOMENTUM_DECAY * momentum + chosen, momentum)
    direction = jnp.where(occupied, chosen + MOMENTUM_DECAY * advanced, 0.0).astype(jnp.bfloat16)
    padded = jnp.concatenate(
        [direction, jnp.zeros((1,) + direction.shape[1:], jnp.bfloat16)], axis=0
    )
    whole = lax.all_gather(padded, "fsdp", axis=1, tiled=True)
    job_slots = jnp.arange(job_count, dtype=jnp.int32) * members + member_here
    job_slots = jnp.where(job_slots < most_slots, job_slots, most_slots)
    full_blocks = jnp.take(whole, job_slots, axis=0)
    result = orthogonalize_all(full_blocks)
    returned = lax.all_to_all(result, "fsdp", split_axis=1, concat_axis=0, tiled=True)
    back_table = np.array(
        [slot % members * job_count + slot // members for slot in range(most_slots)], dtype=np.int32
    )
    group_rows = returned[back_table]
    collected = lax.all_gather(group_rows, "rep", axis=0, tiled=True)
    orthogonal = jnp.take(collected, location, axis=0)
    step_update = orthogonal.astype(jnp.float32) * (0.2 * math.sqrt(block_order))
    new_weight = weight - LEARN_RATE * step_update
    return (step_update, new_weight, advanced)


def solution(mesh):
    return jax.shard_map(
        on_device,
        mesh=mesh,
        in_specs=(P("rep", None, "fsdp", None), P("rep", "fsdp", None), P(None, "fsdp", None), P()),
        out_specs=(P(None, "fsdp", None), P(None, "fsdp", None), P("rep", "fsdp", None)),
        check_vma=False,
    )
```

profile of v0, /device:TPU:1, one launch (start us, length us, event | category | flops | bytes accessed | tf_op | source)
XLA Modules:
  0.0 329.0 jit_solution(942074734531612184)
XLA Ops:
  7.2 0.0 all-reduce.3.cloned.1.call-start
  7.2 0.7 all-reduce.3.cloned.1.call-update
  7.9 0.0 copy-start.1
  7.9 0.0 all-gather.4.cloned.1.call-start
  8.0 0.9 convert_reduce_fusion
  8.9 0.7 compare_and_fusion.1
  9.5 0.2 fusion.25
  9.8 122.2 %all-reduce.3.cloned.1.call-done = bf16[48,16,512]{2,1,0:T(8,128)(2,1)} async-done(((bf16[48,16,512]{2,1,0:T(8,128)(2,1)}), bf16[48,16,512]{2,1,0:T(8,128)(2,1)}) %all-reduce.3.cloned.1.call-update) | async-done | bytes 786448 | tf_op jit(solution)/shard_map/psum | solution.py:66
  132.0 1.3 convert_element_type.141
  133.3 0.6 gather_fusion
  133.9 0.0 copy-done.1
  133.9 0.8 select_convert_fusion
  134.7 0.7 concatenate.3
  135.3 0.0 all-gather.4.cloned.1.call-update
  135.4 74.7 %all-gather.4.cloned.1.call-done = bf16[7,512,512]{2,1,0:T(8,128)(2,1)} async-done(((bf16[7,16,512]{2,1,0:T(8,128)(2,1)}), bf16[7,512,512]{2,1,0:T(8,128)(2,1)}) %all-gather.4.cloned.1.call-update) | async-done | bytes 3670032 | tf_op jit(solution)/shard_map/all_gather | solution.py:75
  210.1 1.9 fusion.11
  212.7 1.7 convolution_convert_fusion.2
  214.4 1.9 fusion.7
  216.3 0.5 convolution_convert_fusion.1
  216.8 0.7 fusion.8
  217.6 0.5 convolution_convert_fusion
  218.0 0.7 fusion.10
  218.8 0.8 copy.14
  219.6 0.5 broadcast.233
  220.1 3.8 %reduce.1 = bf16[512,512]{1,0:T(8,128)(2,1)S(1)} reduce(bf16[512,1,512]{2,1,0:T(2,128)(2,1)S(1)} %bitcast.35, bf16[]{:T(256)} %broadcast.233), dimensions={1}, to_apply=%bitcast.33.reduce_sub_computation | reduce | bytes 1048578
  224.0 1.2 reshape.225
  225.1 8.3 %all-to-all-start = ((bf16[32,2,4096]{2,1,0:T(2,128)(2,1)}), bf16[32,2,4096]{2,1,0:T(2,128)(2,1)S(1)}, u32[]{:S(2)}, u32[]{:S(2)}) async-start(bf16[32,2,4096]{2,1,0:T(2,128)(2,1)} %reshape.225), calls=%async_computation | async-start | bytes 1048576 | tf_op jit(solution)/shard_map/all_to_all | solution.py:80
  233.5 0.0 all-gather.6.cloned.1.call-start
  233.5 33.4 %all-to-all-done = bf16[32,2,4096]{2,1,0:T(2,128)(2,1)S(1)} async-done(((bf16[32,2,4096]{2,1,0:T(2,128)(2,1)}), bf16[32,2,4096]{2,1,0:T(2,128)(2,1)S(1)}, u32[]{:S(2)}, u32[]{:S(2)}) %all-to-all-start) | async-done | bytes 524320 | tf_op jit(solution)/shard_map/all_to_all | solution.py:80
  267.0 0.5 reshape.226
  267.5 0.0 copy-start
  267.5 0.1 copy.12
  267.7 1.2 gather_fusion.1
  268.9 0.0 all-gather.6.cloned.1.call-update
  268.9 49.5 %all-gather.6.cloned.1.call-done = bf16[96,16,512]{2,1,0:T(8,128)(2,1)} async-done(((bf16[6,16,512]{2,1,0:T(8,128)(2,1)}), bf16[96,16,512]{2,1,0:T(8,128)(2,1)}) %all-gather.6.cloned.1.call-update) | async-done | bytes 1572880 | tf_op jit(solution)/shard_map/all_gather | solution.py:85
  318.5 2.0 gather_fusion.2
  320.5 0.0 copy-done
  320.5 2.0 fusion
  (8 shorter events, 0.0 us)
Async XLA Ops:
  7.2 124.8 %all-reduce.3.cloned.1.call-start = ((), (), s32[]{:S(2)}) async-start(), calls=%async_computation.1 | async-start | bytes 1572864 | tf_op jit(solution)/shard_map/psum | solution.py:66
  7.9 126.0 %copy-start.1 = (f32[6,16,512]{2,1,0:T(8,128)S(1)}, f32[6,16,512]{2,1,0:T(8,128)}, u32[]{:S(2)}) copy-start(f32[6,16,512]{2,1,0:T(8,128)} %param.7) | copy-start | bytes 589828
  7.9 202.2 %all-gather.4.cloned.1.call-start = ((), (), s32[]{:S(2)}) async-start(), calls=%async_computation.2 | async-start | bytes 3784704 | tf_op jit(solution)/shard_map/all_gather | solution.py:75
  225.1 41.9 %all-to-all-start = ((bf16[32,2,4096]{2,1,0:T(2,128)(2,1)}), bf16[32,2,4096]{2,1,0:T(2,128)(2,1)S(1)}, u32[]{:S(2)}, u32[]{:S(2)}) async-start(bf16[32,2,4096]{2,1,0:T(2,128)(2,1)} %reshape.225), calls=%async_computation | async-start | bytes 1048576 | tf_op jit(solution)/shard_map/all_to_all | solution.py:80
  233.5 85.0 %all-gather.6.cloned.1.call-start = ((), (), s32[]{:S(2)}) async-start(), calls=%async_computation.3 | async-start | bytes 1671168 | tf_op jit(solution)/shard_map/all_gather | solution.py:85
  267.5 53.0 %copy-start = (f32[48,16,512]{2,1,0:T(8,128)S(1)}, f32[48,16,512]{2,1,0:T(8,128)}, u32[]{:S(2)}) copy-start(f32[48,16,512]{2,1,0:T(8,128)} %param.8) | copy-start | bytes 4718596
Sparse Core Ops, SparseCore 0:
  11.2 120.6 all-reduce.2
  135.5 74.5 all-gather.3
  269.0 49.4 all-gather.5
where the time goes:
time: 329 us
  waiting for transfers between devices  281 us (85%)
  between operations  14.6 us (4%)
  other arithmetic  11.7 us (4%)
  starting transfers between devices  8.46 us (3%)
  local copies, waits for them, and re-layouts  7.59 us (2%)
  matrix products  6.06 us (2%)
    psum x1, waiting for transfers between devices, on_device(): lax.psum(local_parts.astype(jnp.float32).astype(jnp.bfloat16), 'rep')  122 us
    all_gather x1, waiting for transfers between devices, on_device(): whole = lax.all_gather(padded, 'fsdp', axis=1, tiled=True)  74.7 us
    all_gather x1, waiting for transfers between devices, on_device(): collected = lax.all_gather(group_rows, 'rep', axis=0, tiled=True)  49.5 us
    all_to_all x1, waiting for transfers between devices, on_device(): lax.all_to_all(result, 'fsdp', split_axis=1, concat_axis=0, tiled=True)  33.4 us
    all_to_all x1, starting transfers between devices, on_device(): lax.all_to_all(result, 'fsdp', split_axis=1, concat_axis=0, tiled=True)  8.34 us
  transfers between devices with their start and end apart: 4, of which 4 were waited for; matrix products, arithmetic and copies ran while one was open for 1% of the time, Pallas kernels for 0%

commit v1 on v0

v1 whole, which is shorter than its diff:
```python
import functools
import math

import jax
import jax.numpy as jnp
from jax import lax
from jax.experimental import pallas as pl
from jax.experimental.pallas import tpu as pltpu
from jax.sharding import PartitionSpec as P

NS_ITERS = 3
COEF_A = 3.4445
COEF_B = -4.775
COEF_C = 2.0315
MOMENTUM_DECAY = 0.95
LEARN_RATE = 0.02
EPSILON = 1e-07
DIRECTION_SCALE = 1.0 + MOMENTUM_DECAY
FOLD = MOMENTUM_DECAY * MOMENTUM_DECAY / DIRECTION_SCALE
SEGMENT = 4

VMEM = pl.BlockSpec(memory_space=pltpu.VMEM)
SMEM = pl.BlockSpec(memory_space=pltpu.SMEM)


def folded(part, momentum):
    return (part.astype(jnp.float32) + FOLD * momentum).astype(jnp.bfloat16)


def for_owned(owners_ref, here_ref, body):
    here = here_ref[0]

    def step(block, slot):
        mine = owners_ref[block] == here

        @pl.when(mine)
        def _():
            body(block, slot)

        return slot + mine.astype(jnp.int32)

    lax.fori_loop(0, owners_ref.shape[0], step, jnp.int32(0))


def fold_kernel(owners_ref, here_ref, part_ref, momentum_ref, out_ref):
    out_ref[...] = part_ref[...]

    def body(block, slot):
        out_ref[block] = folded(part_ref[block], momentum_ref[slot])

    for_owned(owners_ref, here_ref, body)


def momentum_kernel(owners_ref, here_ref, total_ref, part_ref, momentum_ref, out_ref):
    out_ref[...] = momentum_ref[...]

    def body(block, slot):
        part = part_ref[block].astype(jnp.float32)
        old = momentum_ref[slot]
        added = folded(part_ref[block], old).astype(jnp.float32) - part
        gradient = total_ref[block].astype(jnp.float32) - added
        out_ref[slot] = MOMENTUM_DECAY * old + gradient

    for_owned(owners_ref, here_ref, body)


def sum_kernel(parts_ref, send_ref, total_ref):
    count, blocks = parts_ref.shape[:2]
    for block in range(blocks):
        total = parts_ref[0, block].astype(jnp.float32)
        for source in range(1, count):
            total = total + parts_ref[source, block].astype(jnp.float32)
        total_ref[block] = total.astype(jnp.bfloat16)
        direction = (DIRECTION_SCALE * total).astype(jnp.bfloat16)
        for target in range(send_ref.shape[0]):
            if min(target % SEGMENT, blocks - 1) == block:
                send_ref[target] = direction


def dot_nt(a, b):
    return lax.dot_general(a, b, (((1,), (1,)), ((), ())), preferred_element_type=jnp.float32)


def dot_nn(a, b):
    return jnp.dot(a, b, preferred_element_type=jnp.float32)


def newton_schulz_kernel(segment_ref, own_ref, other_ref, out_ref, x_ref, gram_ref, poly_ref):
    half, order = own_ref.shape
    kept = out_ref.shape[0]
    squares = jnp.float32(0.0)
    for ref in (own_ref, other_ref):
        wide = ref[...].astype(jnp.float32)
        squares = squares + jnp.sum(wide * wide)
    inverse = 1.0 / (jnp.sqrt(squares) + EPSILON)
    x_ref[0:half] = (own_ref[...].astype(jnp.float32) * inverse).astype(jnp.bfloat16)
    x_ref[half:order] = (other_ref[...].astype(jnp.float32) * inverse).astype(jnp.bfloat16)
    tiles = [pl.ds(start, half) for start in range(0, order, half)]
    for iteration in range(NS_ITERS):
        for rows in tiles:
            gram_ref[rows] = dot_nt(x_ref[rows], x_ref[...]).astype(jnp.bfloat16)
        if iteration == NS_ITERS - 1:
            rows = pl.ds(pl.multiple_of(segment_ref[0] * kept, kept), kept)
            gram = gram_ref[rows]
            poly = (COEF_B * gram.astype(jnp.float32) + COEF_C * dot_nn(gram, gram_ref[...])).astype(jnp.bfloat16)
            out_ref[...] = (
                COEF_A * x_ref[rows].astype(jnp.float32) + dot_nn(poly, x_ref[...])
            ).astype(jnp.bfloat16)
            return
        for rows in tiles:
            gram = gram_ref[rows]
            poly_ref[rows] = (
                COEF_B * gram.astype(jnp.float32) + COEF_C * dot_nn(gram, gram_ref[...])
            ).astype(jnp.bfloat16)
        fresh = [
            (COEF_A * x_ref[rows].astype(jnp.float32) + dot_nn(poly_ref[rows], x_ref[...])).astype(jnp.bfloat16)
            for rows in tiles
        ]
        for rows, value in zip(tiles, fresh):
            x_ref[rows] = value


def call(kernel, out_shape, in_specs, scratch=(), flops=0, moved=0):
    return pl.pallas_call(
        kernel,
        out_shape=out_shape,
        in_specs=in_specs,
        out_specs=jax.tree.map(lambda _: VMEM, out_shape),
        scratch_shapes=list(scratch),
        compiler_params=pltpu.CompilerParams(vmem_limit_bytes=24 * 1024 * 1024),
        cost_estimate=pl.CostEstimate(flops=flops, bytes_accessed=moved, transcendentals=0),
    )


def on_device(grad_parts, momentum, weight, owners):
    part = grad_parts[0]
    blocks, rows, order = part.shape
    groups = lax.axis_size("rep")
    members = lax.axis_size("fsdp")
    chips = members // 2
    per_group = blocks // groups
    bf16 = functools.partial(jax.ShapeDtypeStruct, dtype=jnp.bfloat16)
    here = lax.axis_index("rep").astype(jnp.int32).reshape(1)
    segment = (lax.axis_index("fsdp") // (2 * SEGMENT)).astype(jnp.int32).reshape(1)
    same_core = [[2 * chip + core for chip in range(chips)] for core in range(2)]
    same_segment = [
        [2 * (SEGMENT * s + chip) + core for chip in range(SEGMENT)]
        for s in range(chips // SEGMENT)
        for core in range(2)
    ]

    with jax.named_scope("fold_momentum"):
        folded_parts = call(
            fold_kernel, bf16((blocks, rows, order)), [SMEM, SMEM, VMEM, VMEM], moved=1 << 21
        )(owners, here, part, momentum)
    with jax.named_scope("reduce_over_rep"):
        received = lax.all_to_all(
            folded_parts.reshape(groups, per_group, rows, order), "rep", 0, 0, tiled=True
        )
        send, total = call(
            sum_kernel,
            [bf16((chips, rows, order)), bf16((per_group, rows, order))],
            [VMEM],
            moved=1 << 20,
        )(received)
    with jax.named_scope("gather_rows"):
        own = lax.all_to_all(send, "fsdp", 0, 0, axis_index_groups=same_core, tiled=True)
        own = own.reshape(chips * rows, order)
        other = lax.ppermute(own, "fsdp", [(i, i ^ 1) for i in range(members)])
    with jax.named_scope("orthogonalize"):
        square = pltpu.VMEM((order, order), jnp.bfloat16)
        kept = call(
            newton_schulz_kernel,
            bf16((SEGMENT * rows, order)),
            [SMEM, VMEM, VMEM],
            [square] * 3,
            flops=15 * order**3,
            moved=1 << 20,
        )(segment, own, other)
    with jax.named_scope("return_rows"):
        returned = lax.all_to_all(
            kept.reshape(SEGMENT, rows, order), "fsdp", 0, 0, axis_index_groups=same_segment, tiled=True
        )[:per_group]
        collected = lax.all_to_all(
            jnp.broadcast_to(returned[None], (groups, per_group, rows, order)), "rep", 0, 0, tiled=True
        ).reshape(blocks, rows, order)
    with jax.named_scope("update_weight"):
        step_update = collected.astype(jnp.float32) * (0.2 * math.sqrt(order))
        new_weight = weight - LEARN_RATE * step_update
    with jax.named_scope("update_momentum"):
        totals = lax.all_to_all(
            jnp.broadcast_to(total[None], (groups, per_group, rows, order)), "rep", 0, 0, tiled=True
        ).reshape(blocks, rows, order)
        new_momentum = call(
            momentum_kernel,
            jax.ShapeDtypeStruct(momentum.shape, jnp.float32),
            [SMEM, SMEM, VMEM, VMEM, VMEM],
            moved=1 << 21,
        )(owners, here, totals, part, momentum)
    return (step_update, new_weight, new_momentum)


def solution(mesh):
    return jax.shard_map(
        on_device,
        mesh=mesh,
        in_specs=(P("rep", None, "fsdp", None), P("rep", "fsdp", None), P(None, "fsdp", None), P()),
        out_specs=(P(None, "fsdp", None), P(None, "fsdp", None), P("rep", "fsdp", None)),
        check_vma=False,
    )
```

time: 329 us -> 113 us (0.34)
  the two profiles are of different devices: /device:TPU:1 before, /device:TPU:32 now
where the time goes in v1:
time: 113 us; the launch traced here: 112 us
  blocking collectives  62.6 us (55%)
  waiting for transfers between devices  25.8 us (23%)
  starting transfers between devices  9.14 us (8%)
  Pallas kernels  6.52 us (6%)
  local copies, waits for them, and re-layouts  4.68 us (4%)
  other arithmetic  2.92 us (3%)
    all_to_all x1, blocking collectives, on_device(): lax.all_to_all(send, 'fsdp', 0, 0, axis_index_groups=same_core, tiled=True)  32.7 us
    all_to_all x1, blocking collectives, on_device(): lax.all_to_all(folded_parts.reshape(groups, per_group, rows, order), 'rep...  21 us
    all_to_all x1, waiting for transfers between devices, on_device(): lax.all_to_all(jnp.broadcast_to(total[None], (groups, per_group, rows, or...  13.5 us
    all_to_all x1, waiting for transfers between devices, on_device(): lax.all_to_all(jnp.broadcast_to(returned[None], (groups, per_group, rows,...  10.9 us
    all_to_all x1, blocking collectives, on_device(): lax.all_to_all(kept.reshape(SEGMENT, rows, order), 'fsdp', 0, 0, axis_ind...  9.02 us
    all_to_all x1, starting transfers between devices, on_device(): lax.all_to_all(jnp.broadcast_to(returned[None], (groups, per_group, rows,...  3.62 us
    all_to_all x1, starting transfers between devices, on_device(): lax.all_to_all(jnp.broadcast_to(total[None], (groups, per_group, rows, or...  3.61 us
    pallas_call x1, Pallas kernels, on_device(): call(newton_schulz_kernel, bf16((SEGMENT * rows, order)), [SMEM, VMEM, VM...  3.16 us
  transfers between devices with their start and end apart: 3, of which 3 were waited for; matrix products, arithmetic and copies ran while one was open for 0% of the time, Pallas kernels for 2%

profile of v1, /device:TPU:32, one launch (start us, length us, event | category | flops | bytes accessed | tf_op | source)
XLA Modules:
  0.0 112.5 jit_solution(4864354391443019921)
XLA Ops:
  0.6 0.0 copy-start
  0.6 1.1 copy-done
  1.8 0.0 copy-start.2
  1.8 0.9 copy-done.2
  2.7 0.0 copy-start.4
  2.7 0.7 copy-done.4
  3.4 1.3 %fold_momentum.1 = bf16[48,16,512]{2,1,0:T(8,128)(2,1)S(1)} custom-call(s32[48]{0:T(128)S(1)} %copy-done.4, s32[1]{0:T(128)} %bitcast.1.here_ref, bf16[48,16,512]{2,1,0:T(8,128)(2,1)S(1)} %bitcast.10, f32[6,16,512]{2,1,0:T(8,128)S(1)} %copy-done.2), custom_call_target="tpu_custom_call" | custom-call | bytes 2097152 | tf_op jit(solution)/shard_map/fold_momentum/pallas_call | solution.py:153
  4.6 21.0 %all_to_all.25.parts_ref = bf16[16,3,16,512]{3,2,1,0:T(8,128)(2,1)S(1)} all-to-all(bf16[16,3,16,512]{3,2,1,0:T(8,128)(2,1)S(1)} %bitcast.13), channel_id=1, replica_groups=mesh['rep'=16,'fsdp'=32] {'rep'}, dimensions={0} | all-to-all | bytes 1572864 | tf_op jit(solution)/shard_map/reduce_over_rep/all_to_all | solution.py:157
  25.6 0.1 reduce_over_rep.1
  25.7 32.7 %all_to_all.26 = bf16[16,16,512]{2,1,0:T(8,128)(2,1)S(1)} all-to-all(bf16[16,16,512]{2,1,0:T(8,128)(2,1)S(1)} %get-tuple-element.5), channel_id=1, replica_groups={{0,2,4,6,8,10,12,14,16,18,20,22,24,26,28,30},{1,3,5,7,9,11,13,15,17,19,..., dimensions={0} | all-to-all | bytes 524288 | tf_op jit(solution)/shard_map/gather_rows/all_to_all | solution.py:167
  58.4 1.9 %collective-permute-start = (bf16[256,512]{1,0:T(8,128)(2,1)S(1)}, bf16[256,512]{1,0:T(8,128)(2,1)S(1)}, u32[]{:S(2)}, u32[]{:S(2)}) collective-permute-start(bf16[256,512]{1,0:T(8,128)(2,1)S(1)} %bitcast.14), channel_id=1, source_target_pairs={{0,1},{1,0},{2,3},{3,2},{4,5},{5,4},{6,7},{7,6},{8,9},{9,8},{10,11... | collective-permute-start | bytes 786440 | tf_op jit(solution)/shard_map/gather_rows/ppermute | solution.py:169
  60.3 1.5 %collective-permute-done.other_ref = bf16[256,512]{1,0:T(8,128)(2,1)S(1)} collective-permute-done((bf16[256,512]{1,0:T(8,128)(2,1)S(1)}, bf16[256,512]{1,0:T(8,128)(2,1)S(1)}, u32[]{:S(2)}, u32[]{:S(2)}) %collective-permute-start) | collective-permute-done | bytes 262176 | tf_op jit(solution)/shard_map/gather_rows/ppermute | solution.py:169
  61.8 3.2 %orthogonalize.1 = bf16[64,512]{1,0:T(8,128)(2,1)S(1)} custom-call(s32[1]{0:T(128)} %bitcast.segment_ref, bf16[256,512]{1,0:T(8,128)(2,1)S(1)} %bitcast.15, bf16[256,512]{1,0:T(8,128)(2,1)S(1)} %collective-permute-done.other_ref), custom_call_target="tpu_custom_call" | custom-call | flops 2013265920 | bytes 1048576 | tf_op jit(solution)/shard_map/orthogonalize/pallas_call | solution.py:172
  65.0 9.0 %all_to_all.27 = bf16[4,16,512]{2,1,0:T(8,128)(2,1)S(1)} all-to-all(bf16[4,16,512]{2,1,0:T(8,128)(2,1)S(1)} %bitcast.16), channel_id=1, replica_groups={{0,2,4,6},{1,3,5,7},{8,10,12,14},{9,11,13,15},{16,18,20,22},{17,19,21,2..., dimensions={0} | all-to-all | bytes 131072 | tf_op jit(solution)/shard_map/return_rows/all_to_all | solution.py:181
  74.0 1.0 broadcast_in_dim.5
  75.0 3.6 %all-to-all-start.4 = ((bf16[16,3,16,512]{3,2,1,0:T(8,128)(2,1)}), bf16[16,3,16,512]{3,2,1,0:T(8,128)(2,1)S(1)}, u32[]{:S(2)}, u32[]{:S(2)}) async-start(bf16[16,3,16,512]{3,2,1,0:T(8,128)(2,1)} %broadcast_in_dim.5), calls=%async_computation.4 | async-start | bytes 1572864 | tf_op jit(solution)/shard_map/update_momentum/all_to_all | solution.py:191
  78.6 0.0 copy-start.1
  78.6 0.0 copy-start.3
  78.6 0.0 copy-start.5
  78.6 13.5 %all-to-all-done.4 = bf16[16,3,16,512]{3,2,1,0:T(8,128)(2,1)S(1)} async-done(((bf16[16,3,16,512]{3,2,1,0:T(8,128)(2,1)}), bf16[16,3,16,512]{3,2,1,0:T(8,128)(2,1)S(1)}, u32[]{:S(2)}, u32[]{:S(2)}) %all-to-all-start.4) | async-done | bytes 786464 | tf_op jit(solution)/shard_map/update_momentum/all_to_all | solution.py:191
  92.1 1.0 broadcast_in_dim.4
  93.1 3.6 %all-to-all-start.3 = ((bf16[16,3,16,512]{3,2,1,0:T(8,128)(2,1)}), bf16[16,3,16,512]{3,2,1,0:T(8,128)(2,1)S(1)}, u32[]{:S(2)}, u32[]{:S(2)}) async-start(bf16[16,3,16,512]{3,2,1,0:T(8,128)(2,1)} %broadcast_in_dim.4), calls=%async_computation.3 | async-start | bytes 1572864 | tf_op jit(solution)/shard_map/return_rows/all_to_all | solution.py:184
  96.7 0.0 copy-done.1
  96.7 0.0 copy-done.3
  96.7 0.0 copy-done.5
  96.7 2.0 %update_momentum.1 = f32[6,16,512]{2,1,0:T(8,128)} custom-call(s32[48]{0:T(128)S(1)} %copy-done.5, s32[1]{0:T(128)} %bitcast.1.here_ref, bf16[48,16,512]{2,1,0:T(8,128)(2,1)S(1)} %bitcast.12, bf16[48,16,512]{2,1,0:T(8,128)(2,1)S(1)} %bitcast.11, f32[6,16,512]{2,1,0:T(8,128)S(1)} %copy-done.3), custom_call_target="tpu_custom_call" | custom-call | bytes 2097152 | tf_op jit(solution)/shard_map/update_momentum/pallas_call | solution.py:194
  98.7 0.0 copy-start.6
  98.7 10.9 %all-to-all-done.3 = bf16[16,3,16,512]{3,2,1,0:T(8,128)(2,1)S(1)} async-done(((bf16[16,3,16,512]{3,2,1,0:T(8,128)(2,1)}), bf16[16,3,16,512]{3,2,1,0:T(8,128)(2,1)S(1)}, u32[]{:S(2)}, u32[]{:S(2)}) %all-to-all-start.3) | async-done | bytes 786464 | tf_op jit(solution)/shard_map/return_rows/all_to_all | solution.py:184
  109.5 1.4 %convert_multiply_fusion = (f32[16,3,16,512]{3,2,1,0:T(8,128)S(1)}, f32[16,3,16,512]{3,2,1,0:T(8,128)}) fusion(bf16[16,3,16,512]{3,2,1,0:T(8,128)(2,1)S(1)} %all-to-all-done.3), kind=kLoop, calls=%fused_computation | loop fusion | flops 1179648 | bytes 3932160 | tf_op jit(solution)/shard_map/update_weight/mul | solution.py:189
  110.9 0.0 copy-done.6
  110.9 1.5 %bitcast_subtract_fusion = f32[48,16,512]{2,1,0:T(8,128)} fusion(f32[48,16,512]{2,1,0:T(8,128)S(1)} %copy-done.6, f32[16,3,16,512]{3,2,1,0:T(8,128)S(1)} %get-tuple-element.7), kind=kLoop, calls=%fused_computation.2 | loop fusion | flops 393216 | bytes 4718592 | tf_op jit(solution)/shard_map/update_weight/sub | solution.py:189
  (1 shorter events, 0.0 us)
Async XLA Ops:
  0.6 1.1 %copy-start = (bf16[1,48,16,512]{3,2,1,0:T(8,128)(2,1)S(1)}, bf16[1,48,16,512]{3,2,1,0:T(8,128)(2,1)}, u32[]{:S(2)}) copy-start(bf16[1,48,16,512]{3,2,1,0:T(8,128)(2,1)} %param.4) | copy-start | bytes 2359300
  1.8 0.9 copy-start.2
  2.7 0.7 copy-start.4
  58.4 3.4 %collective-permute-start = (bf16[256,512]{1,0:T(8,128)(2,1)S(1)}, bf16[256,512]{1,0:T(8,128)(2,1)S(1)}, u32[]{:S(2)}, u32[]{:S(2)}) collective-permute-start(bf16[256,512]{1,0:T(8,128)(2,1)S(1)} %bitcast.14), channel_id=1, source_target_pairs={{0,1},{1,0},{2,3},{3,2},{4,5},{5,4},{6,7},{7,6},{8,9},{9,8},{10,11... | collective-permute-start | bytes 786440 | tf_op jit(solution)/shard_map/gather_rows/ppermute | solution.py:169
  75.0 17.1 %all-to-all-start.4 = ((bf16[16,3,16,512]{3,2,1,0:T(8,128)(2,1)}), bf16[16,3,16,512]{3,2,1,0:T(8,128)(2,1)S(1)}, u32[]{:S(2)}, u32[]{:S(2)}) async-start(bf16[16,3,16,512]{3,2,1,0:T(8,128)(2,1)} %broadcast_in_dim.5), calls=%async_computation.4 | async-start | bytes 1572864 | tf_op jit(solution)/shard_map/update_momentum/all_to_all | solution.py:191
  78.6 18.1 %copy-start.1 = (bf16[1,48,16,512]{3,2,1,0:T(8,128)(2,1)S(1)}, bf16[1,48,16,512]{3,2,1,0:T(8,128)(2,1)}, u32[]{:S(2)}) copy-start(bf16[1,48,16,512]{3,2,1,0:T(8,128)(2,1)} %param.4) | copy-start | bytes 2359300
  78.6 18.1 %copy-start.3 = (f32[6,16,512]{2,1,0:T(8,128)S(1)}, f32[6,16,512]{2,1,0:T(8,128)}, u32[]{:S(2)}) copy-start(f32[6,16,512]{2,1,0:T(8,128)} %momentum_ref.3) | copy-start | bytes 589828
  78.6 18.1 %copy-start.5 = (s32[48]{0:T(128)S(1)}, s32[48]{0:T(128)}, u32[]{:S(2)}) copy-start(s32[48]{0:T(128)} %owners_ref.3) | copy-start | bytes 580
  93.1 16.5 %all-to-all-start.3 = ((bf16[16,3,16,512]{3,2,1,0:T(8,128)(2,1)}), bf16[16,3,16,512]{3,2,1,0:T(8,128)(2,1)S(1)}, u32[]{:S(2)}, u32[]{:S(2)}) async-start(bf16[16,3,16,512]{3,2,1,0:T(8,128)(2,1)} %broadcast_in_dim.4), calls=%async_computation.3 | async-start | bytes 1572864 | tf_op jit(solution)/shard_map/return_rows/all_to_all | solution.py:184
  98.7 12.3 %copy-start.6 = (f32[48,16,512]{2,1,0:T(8,128)S(1)}, f32[48,16,512]{2,1,0:T(8,128)}, u32[]{:S(2)}) copy-start(f32[48,16,512]{2,1,0:T(8,128)} %param.6) | copy-start | bytes 4718596

commit v2 on v1

--- a/solution.py
+++ b/solution.py
@@ -18,50 +18,93 @@
 DIRECTION_SCALE = 1.0 + MOMENTUM_DECAY
 FOLD = MOMENTUM_DECAY * MOMENTUM_DECAY / DIRECTION_SCALE
 SEGMENT = 4
+PIECES = 6
 
 VMEM = pl.BlockSpec(memory_space=pltpu.VMEM)
 SMEM = pl.BlockSpec(memory_space=pltpu.SMEM)
+HBM = pl.BlockSpec(memory_space=pltpu.HBM)
+
+
+class Table:
+    def __init__(self, blocks, most, per_group):
+        self.block = 0
+        self.own_from = blocks
+        self.own_block = self.own_from + most
+        self.held_owner = self.own_block + most
+        self.count = self.held_owner + per_group
+        self.unused = self.count + 1
+        self.size = 128
 
 
 def folded(part, momentum):
     return (part.astype(jnp.float32) + FOLD * momentum).astype(jnp.bfloat16)
 
 
-def for_owned(owners_ref, here_ref, body):
+def fold_kernel(
+    table,
+    groups,
+    here_ref,
+    owners_hbm,
+    part_hbm,
+    momentum_hbm,
+    out_hbm,
+    table_ref,
+    owners_ref,
+    count_ref,
+    slot_ref,
+    part_ref,
+    momentum_ref,
+    sems,
+):
+    blocks, most = part_ref.shape[0], momentum_ref.shape[0]
+    per_group = blocks // groups
+    copies = [
+        pltpu.make_async_copy(source, target, sems.at[index])
+        for index, (source, target) in enumerate(
+            [(owners_hbm, owners_ref), (part_hbm, part_ref), (momentum_hbm, momentum_ref)]
+        )
+    ]
+    for copy in copies:
+        copy.start()
     here = here_ref[0]
-
-    def step(block, slot):
-        mine = owners_ref[block] == here
-
-        @pl.when(mine)
+    for group in range(groups):
+        count_ref[group] = 0
+    copies[0].wait()
+    for block in range(blocks):
+        owner = owners_ref[block]
+        slot = count_ref[owner]
+        slot_ref[block] = slot
+        count_ref[owner] = slot + 1
+    table_ref[table.count] = count_ref[here]
+    first = jnp.int32(0)
+    for group in range(groups):
+        after = first + count_ref[group]
+        count_ref[group] = first
+        first = after
+    for block in range(blocks):
+        owner, slot = owners_ref[block], slot_ref[block]
+        rank = count_ref[owner] + slot
+        group, place = rank & (groups - 1), rank >> (groups.bit_length() - 1)
+        where = group * SEGMENT + place
+        table_ref[table.block + block] = where
+        mine = owner == here
+        table_ref[jnp.where(mine, table.own_from + slot, table.unused)] = where
+        table_ref[jnp.where(mine, table.own_block + slot, table.unused)] = block
+        table_ref[jnp.where(group == here, table.held_owner + place, table.unused)] = owner
+    for copy in copies[1:]:
+        copy.wait()
+    for slot in range(most):
+
+        @pl.when(slot < table_ref[table.count])
         def _():
-            body(block, slot)
-
-        return slot + mine.astype(jnp.int32)
-
-    lax.fori_loop(0, owners_ref.shape[0], step, jnp.int32(0))
-
-
-def fold_kernel(owners_ref, here_ref, part_ref, momentum_ref, out_ref):
-    out_ref[...] = part_ref[...]
-
-    def body(block, slot):
-        out_ref[block] = folded(part_ref[block], momentum_ref[slot])
-
-    for_owned(owners_ref, here_ref, body)
-
-
-def momentum_kernel(owners_ref, here_ref, total_ref, part_ref, momentum_ref, out_ref):
-    out_ref[...] = momentum_ref[...]
-
-    def body(block, slot):
-        part = part_ref[block].astype(jnp.float32)
-        old = momentum_ref[slot]
-        added = folded(part_ref[block], old).astype(jnp.float32) - part
-        gradient = total_ref[block].astype(jnp.float32) - added
-        out_ref[slot] = MOMENTUM_DECAY * old + gradient
-
-    for_owned(owners_ref, here_ref, body)
+            block = table_ref[table.own_block + slot]
+            part_ref[block] = folded(part_ref[block], momentum_ref[slot])
+
+    for block in range(blocks):
+        where = table_ref[table.block + block]
+        target = (where // SEGMENT) * per_group + (where & (SEGMENT - 1))
+        pltpu.make_async_copy(part_ref.at[block], out_hbm.at[target], sems.at[3]).start()
+    pltpu.make_async_copy(part_ref, out_hbm, sems.at[3]).wait()
 
 
 def sum_kernel(parts_ref, send_ref, total_ref):
@@ -120,14 +163,94 @@
             x_ref[rows] = value
 
 
-def call(kernel, out_shape, in_specs, scratch=(), flops=0, moved=0):
+def spread_kernel(table, table_ref, returned_ref, total_ref, out_ref):
+    per_group = total_ref.shape[0]
+    for place in range(per_group):
+        value = returned_ref[place]
+        for target in range(out_ref.shape[0]):
+            out_ref[target, place] = value
+    for target in range(out_ref.shape[0]):
+        out_ref[target, per_group] = total_ref[0]
+    for place in range(per_group):
+        out_ref[table_ref[table.held_owner + place], per_group] = total_ref[place]
+
+
+def update_kernel(
+    table,
+    scale,
+    table_ref,
+    both_ref,
+    weight_hbm,
+    part_hbm,
+    momentum_hbm,
+    step_hbm,
+    new_hbm,
+    moved_hbm,
+    weight_ref,
+    part_ref,
+    momentum_ref,
+    step_ref,
+    new_ref,
+    moved_ref,
+    sems,
+    slot_sems,
+):
+    blocks, most = weight_ref.shape[0], momentum_ref.shape[0]
+    each = blocks // PIECES
+    chunks = [pl.ds(index * each, each) for index in range(PIECES)]
+    arriving = [
+        pltpu.make_async_copy(weight_hbm.at[chunk], weight_ref.at[chunk], sems.at[index, 0])
+        for index, chunk in enumerate(chunks)
+    ]
+    old = pltpu.make_async_copy(momentum_hbm, momentum_ref, sems.at[PIECES, 0])
+    count = table_ref[table.count]
+    parts = [
+        pltpu.make_async_copy(
+            part_hbm.at[jnp.where(slot < count, table_ref[table.own_block + slot], 0)],
+            part_ref.at[slot],
+            slot_sems.at[slot],
+        )
+        for slot in range(most)
+    ]
+    for copy in arriving + [old] + parts:
+        copy.start()
+    leaving = []
+
+    def leave(source, target, sem):
+        leaving.append(pltpu.make_async_copy(source, target, sem))
+        leaving[-1].start()
+
+    for index, chunk in enumerate(chunks):
+        for block in range(index * each, (index + 1) * each):
+            step_ref[block] = both_ref[table_ref[table.block + block]].astype(jnp.float32) * scale
+        leave(step_ref.at[chunk], step_hbm.at[chunk], sems.at[index, 1])
+    for index, chunk in enumerate(chunks):
+        arriving[index].wait()
+        new_ref[chunk] = weight_ref[chunk] - LEARN_RATE * step_ref[chunk]
+        leave(new_ref.at[chunk], new_hbm.at[chunk], sems.at[index, 2])
+    old.wait()
+    for slot in range(most):
+        parts[slot].wait()
+        part = part_ref[slot]
+        before = momentum_ref[slot]
+        added = folded(part, before).astype(jnp.float32) - part.astype(jnp.float32)
+        used = slot < count
+        source = jnp.where(used, table_ref[table.own_from + slot], 0) | (SEGMENT - 1)
+        gradient = both_ref[source].astype(jnp.float32) - added
+        moved_ref[slot] = jnp.where(used, MOMENTUM_DECAY * before + gradient, before)
+    leave(moved_ref, moved_hbm, sems.at[PIECES, 1])
+    for copy in leaving:
+        copy.wait()
+
+
+def call(kernel, out_shape, in_specs, scratch=(), flops=0, moved=0, out_specs=None, room=40.0):
     return pl.pallas_call(
         kernel,
         out_shape=out_shape,
         in_specs=in_specs,
-        out_specs=jax.tree.map(lambda _: VMEM, out_shape),
+        out_specs=jax.tree.map(lambda _: VMEM, out_shape) if out_specs is None else out_specs,
         scratch_shapes=list(scratch),
-        compiler_params=pltpu.CompilerParams(vmem_limit_bytes=24 * 1024 * 1024),
+        compiler_params=pltpu.CompilerParams(vmem_limit_bytes=int((64 - room) * 1024 * 1024)),
         cost_estimate=pl.CostEstimate(flops=flops, bytes_accessed=moved, transcendentals=0),
     )
 
@@ -135,11 +258,14 @@
 def on_device(grad_parts, momentum, weight, owners):
     part = grad_parts[0]
     blocks, rows, order = part.shape
+    most = momentum.shape[0]
     groups = lax.axis_size("rep")
     members = lax.axis_size("fsdp")
     chips = members // 2
     per_group = blocks // groups
+    table = Table(blocks, most, per_group)
     bf16 = functools.partial(jax.ShapeDtypeStruct, dtype=jnp.bfloat16)
+    f32 = functools.partial(jax.ShapeDtypeStruct, dtype=jnp.float32)
     here = lax.axis_index("rep").astype(jnp.int32).reshape(1)
     segment = (lax.axis_index("fsdp") // (2 * SEGMENT)).astype(jnp.int32).reshape(1)
     same_core = [[2 * chip + core for chip in range(chips)] for core in range(2)]
@@ -150,12 +276,25 @@
     ]
 
     with jax.named_scope("fold_momentum"):
-        folded_parts = call(
-            fold_kernel, bf16((blocks, rows, order)), [SMEM, SMEM, VMEM, VMEM], moved=1 << 21
-        )(owners, here, part, momentum)
+        parts, places = call(
+            functools.partial(fold_kernel, table, groups),
+            [bf16((blocks, rows, order)), jax.ShapeDtypeStruct((table.size,), jnp.int32)],
+            [SMEM, HBM, HBM, HBM],
+            [
+                pltpu.SMEM((blocks,), jnp.int32),
+                pltpu.SMEM((groups,), jnp.int32),
+                pltpu.SMEM((blocks,), jnp.int32),
+                pltpu.VMEM(part.shape, jnp.bfloat16),
+                pltpu.VMEM(momentum.shape, jnp.float32),
+                pltpu.SemaphoreType.DMA((4,)),
+            ],
+            moved=1 << 21,
+            out_specs=[HBM, SMEM],
+            room=1,
+        )(here, owners, part, momentum)
     with jax.named_scope("reduce_over_rep"):
         received = lax.all_to_all(
-            folded_parts.reshape(groups, per_group, rows, order), "rep", 0, 0, tiled=True
+            parts.reshape(groups, per_group, rows, order), "rep", 0, 0, tiled=True
         )
         send, total = call(
             sum_kernel,
@@ -180,24 +319,33 @@
     with jax.named_scope("return_rows"):
         returned = lax.all_to_all(
             kept.reshape(SEGMENT, rows, order), "fsdp", 0, 0, axis_index_groups=same_segment, tiled=True
-        )[:per_group]
-        collected = lax.all_to_all(
-            jnp.broadcast_to(returned[None], (groups, per_group, rows, order)), "rep", 0, 0, tiled=True
-        ).reshape(blocks, rows, order)
-    with jax.named_scope("update_weight"):
-        step_update = collected.astype(jnp.float32) * (0.2 * math.sqrt(order))
-        new_weight = weight - LEARN_RATE * step_update
-    with jax.named_scope("update_momentum"):
-        totals = lax.all_to_all(
-            jnp.broadcast_to(total[None], (groups, per_group, rows, order)), "rep", 0, 0, tiled=True
-        ).reshape(blocks, rows, order)
-        new_momentum = call(
-            momentum_kernel,
-            jax.ShapeDtypeStruct(momentum.shape, jnp.float32),
-            [SMEM, SMEM, VMEM, VMEM, VMEM],
-            moved=1 << 21,
-        )(owners, here, totals, part, momentum)
-    return (step_update, new_weight, new_momentum)
+        )
+        spread = call(
+            functools.partial(spread_kernel, table),
+            bf16((groups, SEGMENT, rows, order)),
+            [SMEM, VMEM, VMEM],
+            moved=1 << 20,
+        )(places, returned, total)
+        both = lax.all_to_all(spread, "rep", 0, 0, tiled=True).reshape(groups * SEGMENT, rows, order)
+    with jax.named_scope("update"):
+        return call(
+            functools.partial(update_kernel, table, 0.2 * math.sqrt(order)),
+            [f32(weight.shape), f32(weight.shape), f32(momentum.shape)],
+            [SMEM, VMEM, HBM, HBM, HBM],
+            [
+                pltpu.VMEM(weight.shape, jnp.float32),
+                pltpu.VMEM((most, rows, order), jnp.bfloat16),
+                pltpu.VMEM(momentum.shape, jnp.float32),
+                pltpu.VMEM(weight.shape, jnp.float32),
+                pltpu.VMEM(weight.shape, jnp.float32),
+                pltpu.VMEM(momentum.shape, jnp.float32),
+                pltpu.SemaphoreType.DMA((PIECES + 1, 3)),
+                pltpu.SemaphoreType.DMA((most,)),
+            ],
+            moved=5 << 20,
+            out_specs=[HBM, HBM, HBM],
+            room=3,
+        )(places, both, weight, part, momentum)
 
 
 def solution(mesh):

time: 113 us -> 97.9 us (0.87)
  the two profiles are of different devices: /device:TPU:32 before, /device:TPU:1 now
where the time goes in v2:
time: 97.9 us; the launch traced here: 96.8 us
  blocking collectives  75.4 us (77%)
  Pallas kernels  10.9 us (11%)
  starting transfers between devices  8.73 us (9%)
  waiting for transfers between devices  1.13 us (1%)
    all_to_all x1, blocking collectives, on_device(): lax.all_to_all(send, 'fsdp', 0, 0, axis_index_groups=same_core, tiled=True)  30.1 us
    all_to_all x1, blocking collectives, on_device(): lax.all_to_all(parts.reshape(groups, per_group, rows, order), 'rep', 0, 0...  18.4 us
    all_to_all x1, blocking collectives, on_device(): lax.all_to_all(spread, 'rep', 0, 0, tiled=True)  18.3 us
    ppermute x1, starting transfers between devices, on_device(): other = lax.ppermute(own, 'fsdp', [(i, i ^ 1) for i in range(members)])  8.73 us
    all_to_all x1, blocking collectives, on_device(): lax.all_to_all(kept.reshape(SEGMENT, rows, order), 'fsdp', 0, 0, axis_ind...  8.64 us
    pallas_call x1, Pallas kernels, on_device(): call(functools.partial(update_kernel, table, 0.2 * math.sqrt(order)), [f3...  4.28 us
    pallas_call x1, Pallas kernels, on_device(): call(newton_schulz_kernel, bf16((SEGMENT * rows, order)), [SMEM, VMEM, VM...  3.16 us
    pallas_call x1, Pallas kernels, on_device(): call(functools.partial(fold_kernel, table, groups), [bf16((blocks, rows,...  2.74 us
  transfers between devices with their start and end apart: 1, of which 1 were waited for; matrix products, arithmetic and copies ran while one was open for 0% of the time, Pallas kernels for 0%

profile of v2, /device:TPU:1, one launch (start us, length us, event | category | flops | bytes accessed | tf_op | source)
XLA Modules:
  0.0 96.8 jit_solution(4113556003459786936)
XLA Ops:
  0.6 2.7 %fold_momentum.1 = (bf16[48,16,512]{2,1,0:T(8,128)(2,1)}, s32[128]{0:T(128)}) custom-call(s32[1]{0:T(128)} %bitcast.here_ref, s32[48]{0:T(128)} %owners_hbm.1, bf16[48,16,512]{2,1,0:T(8,128)(2,1)} %bitcast.11, f32[6,16,512]{2,1,0:T(8,128)} %momentum_hbm.3), custom_call_target="tpu_custom_call" | custom-call | bytes 2097152 | tf_op jit(solution)/shard_map/fold_momentum/pallas_call | solution.py:279
  3.4 18.4 %all_to_all.20.parts_ref = bf16[16,3,16,512]{3,2,1,0:T(8,128)(2,1)S(1)} all-to-all(bf16[16,3,16,512]{3,2,1,0:T(8,128)(2,1)} %bitcast.13), channel_id=1, replica_groups=mesh['rep'=16,'fsdp'=32] {'rep'}, dimensions={0} | all-to-all | bytes 1572864 | tf_op jit(solution)/shard_map/reduce_over_rep/all_to_all | solution.py:296
  21.8 0.1 reduce_over_rep.1
  21.9 30.1 %all_to_all.21 = bf16[16,16,512]{2,1,0:T(8,128)(2,1)S(1)} all-to-all(bf16[16,16,512]{2,1,0:T(8,128)(2,1)S(1)} %get-tuple-element.9), channel_id=1, replica_groups={{0,2,4,6,8,10,12,14,16,18,20,22,24,26,28,30},{1,3,5,7,9,11,13,15,17,19,..., dimensions={0} | all-to-all | bytes 524288 | tf_op jit(solution)/shard_map/gather_rows/all_to_all | solution.py:306
  52.0 8.7 %collective-permute-start = (bf16[256,512]{1,0:T(8,128)(2,1)S(1)}, bf16[256,512]{1,0:T(8,128)(2,1)S(1)}, u32[]{:S(2)}, u32[]{:S(2)}) collective-permute-start(bf16[256,512]{1,0:T(8,128)(2,1)S(1)} %bitcast.7), channel_id=1, source_target_pairs={{0,1},{1,0},{2,3},{3,2},{4,5},{5,4},{6,7},{7,6},{8,9},{9,8},{10,11... | collective-permute-start | bytes 786440 | tf_op jit(solution)/shard_map/gather_rows/ppermute | solution.py:308
  60.7 1.1 %collective-permute-done.other_ref = bf16[256,512]{1,0:T(8,128)(2,1)S(1)} collective-permute-done((bf16[256,512]{1,0:T(8,128)(2,1)S(1)}, bf16[256,512]{1,0:T(8,128)(2,1)S(1)}, u32[]{:S(2)}, u32[]{:S(2)}) %collective-permute-start) | collective-permute-done | bytes 262176 | tf_op jit(solution)/shard_map/gather_rows/ppermute | solution.py:308
  61.8 0.0 copy-start
  61.8 3.2 %orthogonalize.1 = bf16[64,512]{1,0:T(8,128)(2,1)S(1)} custom-call(s32[1]{0:T(128)} %bitcast.2.segment_ref, bf16[256,512]{1,0:T(8,128)(2,1)S(1)} %bitcast.8, bf16[256,512]{1,0:T(8,128)(2,1)S(1)} %collective-permute-done.other_ref), custom_call_target="tpu_custom_call" | custom-call | flops 2013265920 | bytes 1048576 | tf_op jit(solution)/shard_map/orthogonalize/pallas_call | solution.py:311
  65.0 8.6 %all_to_all.22.returned_ref = bf16[4,16,512]{2,1,0:T(8,128)(2,1)S(1)} all-to-all(bf16[4,16,512]{2,1,0:T(8,128)(2,1)S(1)} %bitcast.9), channel_id=1, replica_groups={{0,2,4,6},{1,3,5,7},{8,10,12,14},{9,11,13,15},{16,18,20,22},{17,19,21,2..., dimensions={0} | all-to-all | bytes 131072 | tf_op jit(solution)/shard_map/return_rows/all_to_all | solution.py:320
  73.6 0.0 copy-done
  73.6 0.6 return_rows.1
  74.3 18.3 %all_to_all.23 = bf16[16,4,16,512]{3,2,1,0:T(8,128)(2,1)} all-to-all(bf16[16,4,16,512]{3,2,1,0:T(8,128)(2,1)S(1)} %return_rows.1), channel_id=1, replica_groups=mesh['rep'=16,'fsdp'=32] {'rep'}, dimensions={0} | all-to-all | bytes 2097152 | tf_op jit(solution)/shard_map/return_rows/all_to_all | solution.py:329
  92.5 4.3 %update.1 = (f32[48,16,512]{2,1,0:T(8,128)}, f32[48,16,512]{2,1,0:T(8,128)}, f32[6,16,512]{2,1,0:T(8,128)}) custom-call(s32[128]{0:T(128)} %get-tuple-element.7.table_ref, bf16[64,16,512]{2,1,0:T(8,128)(2,1)} %bitcast.10, f32[48,16,512]{2,1,0:T(8,128)} %weight_hbm.1, bf16[48,16,512]{2,1,0:T(8,128)(2,1)} %bitcast.12, f32[6,16,512]{2,1,0:T(8,128)} %momentum_hbm.3), custom_call_target="tpu_custom_call" | custom-call | bytes 5242880 | tf_op jit(solution)/shard_map/update/pallas_call | solution.py:331
Async XLA Ops:
  52.0 9.9 %collective-permute-start = (bf16[256,512]{1,0:T(8,128)(2,1)S(1)}, bf16[256,512]{1,0:T(8,128)(2,1)S(1)}, u32[]{:S(2)}, u32[]{:S(2)}) collective-permute-start(bf16[256,512]{1,0:T(8,128)(2,1)S(1)} %bitcast.7), channel_id=1, source_target_pairs={{0,1},{1,0},{2,3},{3,2},{4,5},{5,4},{6,7},{7,6},{8,9},{9,8},{10,11... | collective-permute-start | bytes 786440 | tf_op jit(solution)/shard_map/gather_rows/ppermute | solution.py:308
  61.8 11.8 %copy-start = (s32[128]{0:T(128)S(1)}, s32[128]{0:T(128)}, u32[]{:S(2)}) copy-start(s32[128]{0:T(128)} %get-tuple-element.7.table_ref) | copy-start | bytes 1540

commit v3 on v2

--- a/solution.py
+++ b/solution.py
@@ -23,6 +23,7 @@
 VMEM = pl.BlockSpec(memory_space=pltpu.VMEM)
 SMEM = pl.BlockSpec(memory_space=pltpu.SMEM)
 HBM = pl.BlockSpec(memory_space=pltpu.HBM)
+ANY = pl.BlockSpec(memory_space=pl.ANY)
 
 
 class Table:
@@ -48,6 +49,7 @@
     part_hbm,
     momentum_hbm,
     out_hbm,
+    table_hbm,
     table_ref,
     owners_ref,
     count_ref,
@@ -75,12 +77,14 @@
         slot = count_ref[owner]
         slot_ref[block] = slot
         count_ref[owner] = slot + 1
-    table_ref[table.count] = count_ref[here]
+    used = count_ref[here]
+    table_ref[table.count] = used
     first = jnp.int32(0)
     for group in range(groups):
         after = first + count_ref[group]
         count_ref[group] = first
         first = after
+    copies[1].wait()
     for block in range(blocks):
         owner, slot = owners_ref[block], slot_ref[block]
         rank = count_ref[owner] + slot
@@ -91,20 +95,27 @@
         table_ref[jnp.where(mine, table.own_from + slot, table.unused)] = where
         table_ref[jnp.where(mine, table.own_block + slot, table.unused)] = block
         table_ref[jnp.where(group == here, table.held_owner + place, table.unused)] = owner
-    for copy in copies[1:]:
-        copy.wait()
+
+        @pl.when(jnp.logical_not(mine))
+        def _():
+            target = group * per_group + place
+            pltpu.make_async_copy(part_ref.at[block], out_hbm.at[target], sems.at[3]).start()
+
+    table_out = pltpu.make_async_copy(table_ref, table_hbm, sems.at[4])
+    table_out.start()
+    copies[2].wait()
     for slot in range(most):
 
-        @pl.when(slot < table_ref[table.count])
+        @pl.when(slot < used)
         def _():
             block = table_ref[table.own_block + slot]
+            where = table_ref[table.own_from + slot]
+            target = (where >> (SEGMENT.bit_length() - 1)) * per_group + (where & (SEGMENT - 1))
             part_ref[block] = folded(part_ref[block], momentum_ref[slot])
-
-    for block in range(blocks):
-        where = table_ref[table.block + block]
-        target = (where // SEGMENT) * per_group + (where & (SEGMENT - 1))
-        pltpu.make_async_copy(part_ref.at[block], out_hbm.at[target], sems.at[3]).start()
+            pltpu.make_async_copy(part_ref.at[block], out_hbm.at[target], sems.at[3]).start()
+
     pltpu.make_async_copy(part_ref, out_hbm, sems.at[3]).wait()
+    table_out.wait()
 
 
 def sum_kernel(parts_ref, send_ref, total_ref):
@@ -128,49 +139,51 @@
     return jnp.dot(a, b, preferred_element_type=jnp.float32)
 
 
-def newton_schulz_kernel(segment_ref, own_ref, other_ref, out_ref, x_ref, gram_ref, poly_ref):
+def newton_schulz_kernel(segment_ref, own_ref, other_ref, out_ref, x_ref, y_ref, gram_ref, poly_ref):
     half, order = own_ref.shape
     kept = out_ref.shape[0]
-    squares = jnp.float32(0.0)
+    x_ref[0:half] = own_ref[...]
+    x_ref[half:order] = other_ref[...]
+    squares = jnp.zeros((8, order), jnp.float32)
     for ref in (own_ref, other_ref):
         wide = ref[...].astype(jnp.float32)
-        squares = squares + jnp.sum(wide * wide)
-    inverse = 1.0 / (jnp.sqrt(squares) + EPSILON)
-    x_ref[0:half] = (own_ref[...].astype(jnp.float32) * inverse).astype(jnp.bfloat16)
-    x_ref[half:order] = (other_ref[...].astype(jnp.float32) * inverse).astype(jnp.bfloat16)
-    tiles = [pl.ds(start, half) for start in range(0, order, half)]
+        squares = squares + jnp.sum((wide * wide).reshape(half // 8, 8, order), axis=0)
+    inverse = 1.0 / (jnp.sqrt(jnp.sum(squares)) + EPSILON)
+    source_ref, target_ref = x_ref, y_ref
     for iteration in range(NS_ITERS):
-        for rows in tiles:
-            gram_ref[rows] = dot_nt(x_ref[rows], x_ref[...]).astype(jnp.bfloat16)
-        if iteration == NS_ITERS - 1:
-            rows = pl.ds(pl.multiple_of(segment_ref[0] * kept, kept), kept)
-            gram = gram_ref[rows]
-            poly = (COEF_B * gram.astype(jnp.float32) + COEF_C * dot_nn(gram, gram_ref[...])).astype(jnp.bfloat16)
-            out_ref[...] = (
-                COEF_A * x_ref[rows].astype(jnp.float32) + dot_nn(poly, x_ref[...])
-            ).astype(jnp.bfloat16)
-            return
-        for rows in tiles:
-            gram = gram_ref[rows]
-            poly_ref[rows] = (
-                COEF_B * gram.astype(jnp.float32) + COEF_C * dot_nn(gram, gram_ref[...])
-            ).astype(jnp.bfloat16)
-        fresh = [
-            (COEF_A * x_ref[rows].astype(jnp.float32) + dot_nn(poly_ref[rows], x_ref[...])).astype(jnp.bfloat16)
-            for rows in tiles
-        ]
-        for rows, value in zip(tiles, fresh):
-            x_ref[rows] = value
-
-
-def spread_kernel(table, table_ref, returned_ref, total_ref, out_ref):
+        gram = dot_nt(source_ref[...], source_ref[...])
+        if iteration == 0:
+            gram = gram * (inverse * inverse)
+        gram_ref[...] = gram.astype(jnp.bfloat16)
+        last = iteration == NS_ITERS - 1
+        rows = pl.ds(pl.multiple_of(segment_ref[0] * kept, kept), kept) if last else pl.ds(0, order)
+        gram = gram_ref[rows]
+        poly = (COEF_B * gram.astype(jnp.float32) + COEF_C * dot_nn(gram, gram_ref[...])).astype(jnp.bfloat16)
+        if not last:
+            poly_ref[...] = poly
+            poly = poly_ref[...]
+        fresh = COEF_A * source_ref[rows].astype(jnp.float32) + dot_nn(poly, source_ref[...])
+        if iteration == 0:
+            fresh = fresh * inverse
+        if last:
+            out_ref[...] = fresh.astype(jnp.bfloat16)
+        else:
+            target_ref[...] = fresh.astype(jnp.bfloat16)
+            source_ref, target_ref = target_ref, source_ref
+
+
+def spread_kernel(table, table_any, returned_ref, total_ref, out_ref, table_ref, sem):
+    copy = pltpu.make_async_copy(table_any, table_ref, sem)
+    copy.start()
     per_group = total_ref.shape[0]
     for place in range(per_group):
         value = returned_ref[place]
         for target in range(out_ref.shape[0]):
             out_ref[target, place] = value
+    value = total_ref[0]
     for target in range(out_ref.shape[0]):
-        out_ref[target, per_group] = total_ref[0]
+        out_ref[target, per_group] = value
+    copy.wait()
     for place in range(per_group):
         out_ref[table_ref[table.held_owner + place], per_group] = total_ref[place]
 
@@ -180,65 +193,45 @@
     scale,
     table_ref,
     both_ref,
-    weight_hbm,
-    part_hbm,
-    momentum_hbm,
+    weight_ref,
+    part_ref,
+    momentum_ref,
     step_hbm,
     new_hbm,
     moved_hbm,
-    weight_ref,
-    part_ref,
-    momentum_ref,
     step_ref,
     new_ref,
     moved_ref,
     sems,
-    slot_sems,
+    moved_sem,
 ):
     blocks, most = weight_ref.shape[0], momentum_ref.shape[0]
     each = blocks // PIECES
-    chunks = [pl.ds(index * each, each) for index in range(PIECES)]
-    arriving = [
-        pltpu.make_async_copy(weight_hbm.at[chunk], weight_ref.at[chunk], sems.at[index, 0])
-        for index, chunk in enumerate(chunks)
-    ]
-    old = pltpu.make_async_copy(momentum_hbm, momentum_ref, sems.at[PIECES, 0])
-    count = table_ref[table.count]
-    parts = [
-        pltpu.make_async_copy(
-            part_hbm.at[jnp.where(slot < count, table_ref[table.own_block + slot], 0)],
-            part_ref.at[slot],
-            slot_sems.at[slot],
-        )
-        for slot in range(most)
-    ]
-    for copy in arriving + [old] + parts:
-        copy.start()
     leaving = []
 
     def leave(source, target, sem):
         leaving.append(pltpu.make_async_copy(source, target, sem))
         leaving[-1].start()
 
-    for index, chunk in enumerate(chunks):
+    for index in range(PIECES):
+        chunk = pl.ds(index * each, each)
         for block in range(index * each, (index + 1) * each):
-            step_ref[block] = both_ref[table_ref[table.block + block]].astype(jnp.float32) * scale
-        leave(step_ref.at[chunk], step_hbm.at[chunk], sems.at[index, 1])
-    for index, chunk in enumerate(chunks):
-        arriving[index].wait()
-        new_ref[chunk] = weight_ref[chunk] - LEARN_RATE * step_ref[chunk]
-        leave(new_ref.at[chunk], new_hbm.at[chunk], sems.at[index, 2])
-    old.wait()
+            step = both_ref[table_ref[table.block + block]].astype(jnp.float32) * scale
+            step_ref[block] = step
+            new_ref[block] = weight_ref[block] - LEARN_RATE * step
+        leave(step_ref.at[chunk], step_hbm.at[chunk], sems.at[index, 0])
+        leave(new_ref.at[chunk], new_hbm.at[chunk], sems.at[index, 1])
+    count = table_ref[table.count]
     for slot in range(most):
-        parts[slot].wait()
-        part = part_ref[slot]
+        used = slot < count
+        block = jnp.where(used, table_ref[table.own_block + slot], 0)
+        source = jnp.where(used, table_ref[table.own_from + slot], 0) | (SEGMENT - 1)
+        part = part_ref[block]
         before = momentum_ref[slot]
         added = folded(part, before).astype(jnp.float32) - part.astype(jnp.float32)
-        used = slot < count
-        source = jnp.where(used, table_ref[table.own_from + slot], 0) | (SEGMENT - 1)
         gradient = both_ref[source].astype(jnp.float32) - added
         moved_ref[slot] = jnp.where(used, MOMENTUM_DECAY * before + gradient, before)
-    leave(moved_ref, moved_hbm, sems.at[PIECES, 1])
+    leave(moved_ref, moved_hbm, moved_sem)
     for copy in leaving:
         copy.wait()
 
@@ -281,15 +274,16 @@
             [bf16((blocks, rows, order)), jax.ShapeDtypeStruct((table.size,), jnp.int32)],
             [SMEM, HBM, HBM, HBM],
             [
+                pltpu.SMEM((table.size,), jnp.int32),
                 pltpu.SMEM((blocks,), jnp.int32),
                 pltpu.SMEM((groups,), jnp.int32),
                 pltpu.SMEM((blocks,), jnp.int32),
                 pltpu.VMEM(part.shape, jnp.bfloat16),
                 pltpu.VMEM(momentum.shape, jnp.float32),
-                pltpu.SemaphoreType.DMA((4,)),
+                pltpu.SemaphoreType.DMA((5,)),
             ],
             moved=1 << 21,
-            out_specs=[HBM, SMEM],
+            out_specs=[HBM, HBM],
             room=1,
         )(here, owners, part, momentum)
     with jax.named_scope("reduce_over_rep"):
@@ -312,7 +306,7 @@
             newton_schulz_kernel,
             bf16((SEGMENT * rows, order)),
             [SMEM, VMEM, VMEM],
-            [square] * 3,
+            [square] * 4,
             flops=15 * order**3,
             moved=1 << 20,
         )(segment, own, other)
@@ -323,7 +317,8 @@
         spread = call(
             functools.partial(spread_kernel, table),
             bf16((groups, SEGMENT, rows, order)),
-            [SMEM, VMEM, VMEM],
+            [ANY, VMEM, VMEM],
+            [pltpu.SMEM((table.size,), jnp.int32), pltpu.SemaphoreType.DMA],
             moved=1 << 20,
         )(places, returned, total)
         both = lax.all_to_all(spread, "rep", 0, 0, tiled=True).reshape(groups * SEGMENT, rows, order)
@@ -331,20 +326,16 @@
         return call(
             functools.partial(update_kernel, table, 0.2 * math.sqrt(order)),
             [f32(weight.shape), f32(weight.shape), f32(momentum.shape)],
-            [SMEM, VMEM, HBM, HBM, HBM],
+            [SMEM, VMEM, VMEM, VMEM, VMEM],
             [
-                pltpu.VMEM(weight.shape, jnp.float32),
-                pltpu.VMEM((most, rows, order), jnp.bfloat16),
-                pltpu.VMEM(momentum.shape, jnp.float32),
                 pltpu.VMEM(weight.shape, jnp.float32),
                 pltpu.VMEM(weight.shape, jnp.float32),
                 pltpu.VMEM(momentum.shape, jnp.float32),
-                pltpu.SemaphoreType.DMA((PIECES + 1, 3)),
-                pltpu.SemaphoreType.DMA((most,)),
+                pltpu.SemaphoreType.DMA((PIECES, 2)),
+                pltpu.SemaphoreType.DMA,
             ],
             moved=5 << 20,
             out_specs=[HBM, HBM, HBM],
-            room=3,
         )(places, both, weight, part, momentum)
 
 

time: 97.9 us -> 94.8 us (0.968)
  Pallas kernels: 10.9 us -> 7.96 us
    pallas_call x1, Pallas kernels: 4.28 us -> 2.4 us  [on_device(): call(functools.partial(update_kernel, table, 0.2 * math.sqrt(order)), [f3...]
where the time goes in v3:
time: 94.8 us; the launch traced here: 93.8 us
  blocking collectives  75.3 us (79%)
  starting transfers between devices  8.73 us (9%)
  Pallas kernels  7.96 us (8%)
  waiting for transfers between devices  1.13 us (1%)
    all_to_all x1, blocking collectives, on_device(): lax.all_to_all(send, 'fsdp', 0, 0, axis_index_groups=same_core, tiled=True)  30.2 us
    all_to_all x1, blocking collectives, on_device(): lax.all_to_all(parts.reshape(groups, per_group, rows, order), 'rep', 0, 0...  18.3 us
    all_to_all x1, blocking collectives, on_device(): lax.all_to_all(spread, 'rep', 0, 0, tiled=True)  18.2 us
    ppermute x1, starting transfers between devices, on_device(): other = lax.ppermute(own, 'fsdp', [(i, i ^ 1) for i in range(members)])  8.73 us
    all_to_all x1, blocking collectives, on_device(): lax.all_to_all(kept.reshape(SEGMENT, rows, order), 'fsdp', 0, 0, axis_ind...  8.64 us
    pallas_call x1, Pallas kernels, on_device(): call(newton_schulz_kernel, bf16((SEGMENT * rows, order)), [SMEM, VMEM, VM...  2.79 us
    pallas_call x1, Pallas kernels, on_device(): call(functools.partial(update_kernel, table, 0.2 * math.sqrt(order)), [f3...  2.4 us
    pallas_call x1, Pallas kernels, on_device(): call(functools.partial(fold_kernel, table, groups), [bf16((blocks, rows,...  2.09 us
  transfers between devices with their start and end apart: 1, of which 1 were waited for; matrix products, arithmetic and copies ran while one was open for 0% of the time, Pallas kernels for 0%

profile of v3, /device:TPU:1, one launch (start us, length us, event | category | flops | bytes accessed | tf_op | source)
XLA Modules:
  0.0 93.8 jit_solution(12441632826257936977)
XLA Ops:
  0.6 2.1 %fold_momentum.1 = (bf16[48,16,512]{2,1,0:T(8,128)(2,1)}, s32[128]{0:T(128)}) custom-call(s32[1]{0:T(128)} %bitcast.here_ref, s32[48]{0:T(128)} %owners_hbm.1, bf16[48,16,512]{2,1,0:T(8,128)(2,1)} %bitcast.8, f32[6,16,512]{2,1,0:T(8,128)} %momentum_ref.1), custom_call_target="tpu_custom_call" | custom-call | bytes 2097152 | tf_op jit(solution)/shard_map/fold_momentum/pallas_call | solution.py:272
  2.7 18.3 %all_to_all.20.parts_ref = bf16[16,3,16,512]{3,2,1,0:T(8,128)(2,1)S(1)} all-to-all(bf16[16,3,16,512]{3,2,1,0:T(8,128)(2,1)} %bitcast.13), channel_id=1, replica_groups=mesh['rep'=16,'fsdp'=32] {'rep'}, dimensions={0} | all-to-all | bytes 1572864 | tf_op jit(solution)/shard_map/reduce_over_rep/all_to_all | solution.py:290
  21.0 0.1 reduce_over_rep.1
  21.1 30.2 %all_to_all.21 = bf16[16,16,512]{2,1,0:T(8,128)(2,1)S(1)} all-to-all(bf16[16,16,512]{2,1,0:T(8,128)(2,1)S(1)} %get-tuple-element.9), channel_id=1, replica_groups={{0,2,4,6,8,10,12,14,16,18,20,22,24,26,28,30},{1,3,5,7,9,11,13,15,17,19,..., dimensions={0} | all-to-all | bytes 524288 | tf_op jit(solution)/shard_map/gather_rows/all_to_all | solution.py:300
  51.3 8.7 %collective-permute-start = (bf16[256,512]{1,0:T(8,128)(2,1)S(1)}, bf16[256,512]{1,0:T(8,128)(2,1)S(1)}, u32[]{:S(2)}, u32[]{:S(2)}) collective-permute-start(bf16[256,512]{1,0:T(8,128)(2,1)S(1)} %bitcast.10), channel_id=1, source_target_pairs={{0,1},{1,0},{2,3},{3,2},{4,5},{5,4},{6,7},{7,6},{8,9},{9,8},{10,11... | collective-permute-start | bytes 786440 | tf_op jit(solution)/shard_map/gather_rows/ppermute | solution.py:302
  60.0 1.1 %collective-permute-done.other_ref = bf16[256,512]{1,0:T(8,128)(2,1)S(1)} collective-permute-done((bf16[256,512]{1,0:T(8,128)(2,1)S(1)}, bf16[256,512]{1,0:T(8,128)(2,1)S(1)}, u32[]{:S(2)}, u32[]{:S(2)}) %collective-permute-start) | collective-permute-done | bytes 262176 | tf_op jit(solution)/shard_map/gather_rows/ppermute | solution.py:302
  61.2 0.0 copy-start.3
  61.2 2.8 %orthogonalize.1 = bf16[64,512]{1,0:T(8,128)(2,1)S(1)} custom-call(s32[1]{0:T(128)} %bitcast.2.segment_ref, bf16[256,512]{1,0:T(8,128)(2,1)S(1)} %bitcast.11, bf16[256,512]{1,0:T(8,128)(2,1)S(1)} %collective-permute-done.other_ref), custom_call_target="tpu_custom_call" | custom-call | flops 2013265920 | bytes 1048576 | tf_op jit(solution)/shard_map/orthogonalize/pallas_call | solution.py:305
  64.0 8.6 %all_to_all.22.returned_ref = bf16[4,16,512]{2,1,0:T(8,128)(2,1)S(1)} all-to-all(bf16[4,16,512]{2,1,0:T(8,128)(2,1)S(1)} %bitcast.12), channel_id=1, replica_groups={{0,2,4,6},{1,3,5,7},{8,10,12,14},{9,11,13,15},{16,18,20,22},{17,19,21,2..., dimensions={0} | all-to-all | bytes 131072 | tf_op jit(solution)/shard_map/return_rows/all_to_all | solution.py:314
  72.6 0.0 copy-done.3
  72.6 0.0 copy-start
  72.6 0.0 copy-start.1
  72.6 0.0 copy-start.2
  72.6 0.6 return_rows.1
  73.2 18.2 %all_to_all.23 = bf16[16,4,16,512]{3,2,1,0:T(8,128)(2,1)S(1)} all-to-all(bf16[16,4,16,512]{3,2,1,0:T(8,128)(2,1)S(1)} %return_rows.1), channel_id=1, replica_groups=mesh['rep'=16,'fsdp'=32] {'rep'}, dimensions={0} | all-to-all | bytes 2097152 | tf_op jit(solution)/shard_map/return_rows/all_to_all | solution.py:324
  91.4 0.0 copy-done
  91.4 0.0 copy-done.1
  91.4 0.0 copy-done.2
  91.4 2.4 %update.1 = (f32[48,16,512]{2,1,0:T(8,128)}, f32[48,16,512]{2,1,0:T(8,128)}, f32[6,16,512]{2,1,0:T(8,128)}) custom-call(s32[128]{0:T(128)S(1)} %copy-done.3, bf16[64,16,512]{2,1,0:T(8,128)(2,1)S(1)} %bitcast.7, f32[48,16,512]{2,1,0:T(8,128)S(1)} %copy-done.1, bf16[48,16,512]{2,1,0:T(8,128)(2,1)S(1)} %bitcast.9, f32[6,16,512]{2,1,0:T(8,128)S(1)} %copy-done.2), custom_call_target="tpu_custom_call" | custom-call | bytes 5242880 | tf_op jit(solution)/shard_map/update/pallas_call | solution.py:326
Async XLA Ops:
  51.3 9.9 %collective-permute-start = (bf16[256,512]{1,0:T(8,128)(2,1)S(1)}, bf16[256,512]{1,0:T(8,128)(2,1)S(1)}, u32[]{:S(2)}, u32[]{:S(2)}) collective-permute-start(bf16[256,512]{1,0:T(8,128)(2,1)S(1)} %bitcast.10), channel_id=1, source_target_pairs={{0,1},{1,0},{2,3},{3,2},{4,5},{5,4},{6,7},{7,6},{8,9},{9,8},{10,11... | collective-permute-start | bytes 786440 | tf_op jit(solution)/shard_map/gather_rows/ppermute | solution.py:302
  61.2 11.4 %copy-start.3 = (s32[128]{0:T(128)S(1)}, s32[128]{0:T(128)}, u32[]{:S(2)}) copy-start(s32[128]{0:T(128)} %get-tuple-element.7.table_any.table_ref) | copy-start | bytes 1540
  72.6 18.8 %copy-start = (bf16[1,48,16,512]{3,2,1,0:T(8,128)(2,1)S(1)}, bf16[1,48,16,512]{3,2,1,0:T(8,128)(2,1)}, u32[]{:S(2)}) copy-start(bf16[1,48,16,512]{3,2,1,0:T(8,128)(2,1)} %param.4) | copy-start | bytes 2359300
  72.6 18.8 %copy-start.1 = (f32[48,16,512]{2,1,0:T(8,128)S(1)}, f32[48,16,512]{2,1,0:T(8,128)}, u32[]{:S(2)}) copy-start(f32[48,16,512]{2,1,0:T(8,128)} %weight_ref.1) | copy-start | bytes 4718596
  72.6 18.8 %copy-start.2 = (f32[6,16,512]{2,1,0:T(8,128)S(1)}, f32[6,16,512]{2,1,0:T(8,128)}, u32[]{:S(2)}) copy-start(f32[6,16,512]{2,1,0:T(8,128)} %momentum_ref.1) | copy-start | bytes 589828

commit v4 on v3

--- a/solution.py
+++ b/solution.py
@@ -26,34 +26,54 @@
 ANY = pl.BlockSpec(memory_space=pl.ANY)
 
 
-class Table:
-    def __init__(self, blocks, most, per_group):
-        self.block = 0
-        self.own_from = blocks
-        self.own_block = self.own_from + most
-        self.held_owner = self.own_block + most
-        self.count = self.held_owner + per_group
-        self.unused = self.count + 1
-        self.size = 128
-
-
 def folded(part, momentum):
     return (part.astype(jnp.float32) + FOLD * momentum).astype(jnp.bfloat16)
 
 
+def rank_blocks(groups, owners_ref, ranks_ref):
+    blocks = owners_ref.shape[0]
+    for group in range(groups):
+        ranks_ref[blocks + group] = 0
+    for block in range(blocks):
+        owner = owners_ref[block]
+        slot = ranks_ref[blocks + owner]
+        ranks_ref[block] = slot
+        ranks_ref[blocks + owner] = slot + 1
+    first = jnp.int32(0)
+    for group in range(groups):
+        after = first + ranks_ref[blocks + group]
+        ranks_ref[blocks + group] = first
+        first = after
+    for block in range(blocks):
+        ranks_ref[block] = ranks_ref[blocks + owners_ref[block]] + ranks_ref[block]
+
+
+def split_rank(groups, rank):
+    return rank & (groups - 1), rank >> (groups.bit_length() - 1)
+
+
+def list_owned(blocks, groups, here, ranks_ref, owned_ref):
+    first = ranks_ref[blocks + here]
+    after = jnp.where(here == groups - 1, blocks, ranks_ref[blocks + jnp.minimum(here + 1, groups - 1)])
+    count = after - first
+    unused = owned_ref.shape[0] - 1
+    for block in range(blocks):
+        slot = ranks_ref[block] - first
+        owned_ref[jnp.where((slot >= 0) & (slot < count), slot, unused)] = block
+    return first, count
+
+
 def fold_kernel(
-    table,
     groups,
     here_ref,
     owners_hbm,
     part_hbm,
     momentum_hbm,
-    out_hbm,
-    table_hbm,
-    table_ref,
+    out_ref,
+    ranks_out_ref,
     owners_ref,
-    count_ref,
-    slot_ref,
+    ranks_ref,
+    owned_ref,
     part_ref,
     momentum_ref,
     sems,
@@ -68,54 +88,28 @@
     ]
     for copy in copies:
         copy.start()
-    here = here_ref[0]
-    for group in range(groups):
-        count_ref[group] = 0
     copies[0].wait()
-    for block in range(blocks):
-        owner = owners_ref[block]
-        slot = count_ref[owner]
-        slot_ref[block] = slot
-        count_ref[owner] = slot + 1
-    used = count_ref[here]
-    table_ref[table.count] = used
-    first = jnp.int32(0)
-    for group in range(groups):
-        after = first + count_ref[group]
-        count_ref[group] = first
-        first = after
+    rank_blocks(groups, owners_ref, ranks_ref)
+    ranks_out = pltpu.make_async_copy(ranks_ref, ranks_out_ref, sems.at[3])
+    ranks_out.start()
+    _, count = list_owned(blocks, groups, here_ref[0], ranks_ref, owned_ref)
+
+    def target_of(block):
+        group, place = split_rank(groups, ranks_ref[block])
+        return group * per_group + place
+
     copies[1].wait()
     for block in range(blocks):
-        owner, slot = owners_ref[block], slot_ref[block]
-        rank = count_ref[owner] + slot
-        group, place = rank & (groups - 1), rank >> (groups.bit_length() - 1)
-        where = group * SEGMENT + place
-        table_ref[table.block + block] = where
-        mine = owner == here
-        table_ref[jnp.where(mine, table.own_from + slot, table.unused)] = where
-        table_ref[jnp.where(mine, table.own_block + slot, table.unused)] = block
-        table_ref[jnp.where(group == here, table.held_owner + place, table.unused)] = owner
-
-        @pl.when(jnp.logical_not(mine))
-        def _():
-            target = group * per_group + place
-            pltpu.make_async_copy(part_ref.at[block], out_hbm.at[target], sems.at[3]).start()
-
-    table_out = pltpu.make_async_copy(table_ref, table_hbm, sems.at[4])
-    table_out.start()
+        out_ref[target_of(block)] = part_ref[block]
     copies[2].wait()
     for slot in range(most):
 
-        @pl.when(slot < used)
+        @pl.when(slot < count)
         def _():
-            block = table_ref[table.own_block + slot]
-            where = table_ref[table.own_from + slot]
-            target = (where >> (SEGMENT.bit_length() - 1)) * per_group + (where & (SEGMENT - 1))
-            part_ref[block] = folded(part_ref[block], momentum_ref[slot])
-            pltpu.make_async_copy(part_ref.at[block], out_hbm.at[target], sems.at[3]).start()
-
-    pltpu.make_async_copy(part_ref, out_hbm, sems.at[3]).wait()
-    table_out.wait()
+            block = owned_ref[slot]
+            out_ref[target_of(block)] = folded(part_ref[block], momentum_ref[slot])
+
+    ranks_out.wait()
 
 
 def sum_kernel(parts_ref, send_ref, total_ref):
@@ -172,26 +166,32 @@
             source_ref, target_ref = target_ref, source_ref
 
 
-def spread_kernel(table, table_any, returned_ref, total_ref, out_ref, table_ref, sem):
-    copy = pltpu.make_async_copy(table_any, table_ref, sem)
+def spread_kernel(groups, here_ref, ranks_any, returned_ref, total_ref, out_ref, ranks_ref, sem):
+    copy = pltpu.make_async_copy(ranks_any, ranks_ref, sem)
     copy.start()
     per_group = total_ref.shape[0]
+    blocks = groups * per_group
     for place in range(per_group):
         value = returned_ref[place]
-        for target in range(out_ref.shape[0]):
+        for target in range(groups):
             out_ref[target, place] = value
     value = total_ref[0]
-    for target in range(out_ref.shape[0]):
+    for target in range(groups):
         out_ref[target, per_group] = value
     copy.wait()
     for place in range(per_group):
-        out_ref[table_ref[table.held_owner + place], per_group] = total_ref[place]
+        rank = place * groups + here_ref[0]
+        owner = jnp.int32(-1)
+        for group in range(groups):
+            owner = owner + (ranks_ref[blocks + group] <= rank).astype(jnp.int32)
+        out_ref[owner, per_group] = total_ref[place]
 
 
 def update_kernel(
-    table,
+    groups,
     scale,
-    table_ref,
+    here_ref,
+    ranks_ref,
     both_ref,
     weight_ref,
     part_ref,
@@ -199,6 +199,7 @@
     step_hbm,
     new_hbm,
     moved_hbm,
+    owned_ref,
     step_ref,
     new_ref,
     moved_ref,
@@ -206,6 +207,7 @@
     moved_sem,
 ):
     blocks, most = weight_ref.shape[0], momentum_ref.shape[0]
+    per_group = blocks // groups
     each = blocks // PIECES
     leaving = []
 
@@ -216,20 +218,21 @@
     for index in range(PIECES):
         chunk = pl.ds(index * each, each)
         for block in range(index * each, (index + 1) * each):
-            step = both_ref[table_ref[table.block + block]].astype(jnp.float32) * scale
+            group, place = split_rank(groups, ranks_ref[block])
+            step = both_ref[group, place].astype(jnp.float32) * scale
             step_ref[block] = step
             new_ref[block] = weight_ref[block] - LEARN_RATE * step
         leave(step_ref.at[chunk], step_hbm.at[chunk], sems.at[index, 0])
         leave(new_ref.at[chunk], new_hbm.at[chunk], sems.at[index, 1])
-    count = table_ref[table.count]
+    first, count = list_owned(blocks, groups, here_ref[0], ranks_ref, owned_ref)
     for slot in range(most):
         used = slot < count
-        block = jnp.where(used, table_ref[table.own_block + slot], 0)
-        source = jnp.where(used, table_ref[table.own_from + slot], 0) | (SEGMENT - 1)
+        block = jnp.where(used, owned_ref[slot], 0)
+        group, _ = split_rank(groups, first + slot)
         part = part_ref[block]
         before = momentum_ref[slot]
         added = folded(part, before).astype(jnp.float32) - part.astype(jnp.float32)
-        gradient = both_ref[source].astype(jnp.float32) - added
+        gradient = both_ref[group, per_group].astype(jnp.float32) - added
         moved_ref[slot] = jnp.where(used, MOMENTUM_DECAY * before + gradient, before)
     leave(moved_ref, moved_hbm, moved_sem)
     for copy in leaving:
@@ -256,7 +259,7 @@
     members = lax.axis_size("fsdp")
     chips = members // 2
     per_group = blocks // groups
-    table = Table(blocks, most, per_group)
+    ranks_size = blocks + groups
     bf16 = functools.partial(jax.ShapeDtypeStruct, dtype=jnp.bfloat16)
     f32 = functools.partial(jax.ShapeDtypeStruct, dtype=jnp.float32)
     here = lax.axis_index("rep").astype(jnp.int32).reshape(1)
@@ -269,23 +272,20 @@
     ]
 
     with jax.named_scope("fold_momentum"):
-        parts, places = call(
-            functools.partial(fold_kernel, table, groups),
-            [bf16((blocks, rows, order)), jax.ShapeDtypeStruct((table.size,), jnp.int32)],
+        parts, ranks = call(
+            functools.partial(fold_kernel, groups),
+            [pltpu.VMEM((blocks, rows, order), jnp.bfloat16), pltpu.VMEM((ranks_size,), jnp.int32)],
             [SMEM, HBM, HBM, HBM],
             [
-                pltpu.SMEM((table.size,), jnp.int32),
                 pltpu.SMEM((blocks,), jnp.int32),
-                pltpu.SMEM((groups,), jnp.int32),
-                pltpu.SMEM((blocks,), jnp.int32),
+                pltpu.SMEM((ranks_size,), jnp.int32),
+                pltpu.SMEM((most + 1,), jnp.int32),
                 pltpu.VMEM(part.shape, jnp.bfloat16),
                 pltpu.VMEM(momentum.shape, jnp.float32),
-                pltpu.SemaphoreType.DMA((5,)),
+                pltpu.SemaphoreType.DMA((4,)),
             ],
             moved=1 << 21,
-            out_specs=[HBM, HBM],
-            room=1,
-        )(here, owners, part, momentum)
+        )(here, *(pltpu.with_memory_space_constraint(array, pltpu.HBM) for array in (owners, part, momentum)))
     with jax.named_scope("reduce_over_rep"):
         received = lax.all_to_all(
             parts.reshape(groups, per_group, rows, order), "rep", 0, 0, tiled=True
@@ -315,19 +315,20 @@
             kept.reshape(SEGMENT, rows, order), "fsdp", 0, 0, axis_index_groups=same_segment, tiled=True
         )
         spread = call(
-            functools.partial(spread_kernel, table),
-            bf16((groups, SEGMENT, rows, order)),
-            [ANY, VMEM, VMEM],
-            [pltpu.SMEM((table.size,), jnp.int32), pltpu.SemaphoreType.DMA],
+            functools.partial(spread_kernel, groups),
+            bf16((groups, per_group + 1, rows, order)),
+            [SMEM, ANY, VMEM, VMEM],
+            [pltpu.SMEM((ranks_size,), jnp.int32), pltpu.SemaphoreType.DMA],
             moved=1 << 20,
-        )(places, returned, total)
-        both = lax.all_to_all(spread, "rep", 0, 0, tiled=True).reshape(groups * SEGMENT, rows, order)
+        )(here, ranks, returned, total)
+        both = lax.all_to_all(spread, "rep", 0, 0, tiled=True)
     with jax.named_scope("update"):
         return call(
-            functools.partial(update_kernel, table, 0.2 * math.sqrt(order)),
+            functools.partial(update_kernel, groups, 0.2 * math.sqrt(order)),
             [f32(weight.shape), f32(weight.shape), f32(momentum.shape)],
-            [SMEM, VMEM, VMEM, VMEM, VMEM],
+            [SMEM, SMEM, VMEM, VMEM, VMEM, VMEM],
             [
+                pltpu.SMEM((most + 1,), jnp.int32),
                 pltpu.VMEM(weight.shape, jnp.float32),
                 pltpu.VMEM(weight.shape, jnp.float32),
                 pltpu.VMEM(momentum.shape, jnp.float32),
@@ -336,7 +337,7 @@
             ],
             moved=5 << 20,
             out_specs=[HBM, HBM, HBM],
-        )(places, both, weight, part, momentum)
+        )(here, ranks, both, weight, part, momentum)
 
 
 def solution(mesh):

time: 94.8 us -> 94.2 us (level)
    all_to_all x1, blocking collectives: 30.2 us -> 29.1 us  [on_device(): lax.all_to_all(send, 'fsdp', 0, 0, axis_index_groups=same_core, tiled=True)]
where the time goes in v4:
time: 94.2 us; the launch traced here: 93.3 us
  blocking collectives  75.1 us (80%)
  starting transfers between devices  8.73 us (9%)
  Pallas kernels  7.65 us (8%)
  waiting for transfers between devices  1.13 us (1%)
    all_to_all x1, blocking collectives, on_device(): lax.all_to_all(send, 'fsdp', 0, 0, axis_index_groups=same_core, tiled=True)  29.1 us
    all_to_all x1, blocking collectives, on_device(): lax.all_to_all(parts.reshape(groups, per_group, rows, order), 'rep', 0, 0...  19.1 us
    all_to_all x1, blocking collectives, on_device(): both = lax.all_to_all(spread, 'rep', 0, 0, tiled=True)  18.2 us
    ppermute x1, starting transfers between devices, on_device(): other = lax.ppermute(own, 'fsdp', [(i, i ^ 1) for i in range(members)])  8.73 us
    all_to_all x1, blocking collectives, on_device(): lax.all_to_all(kept.reshape(SEGMENT, rows, order), 'fsdp', 0, 0, axis_ind...  8.64 us
    pallas_call x1, Pallas kernels, on_device(): call(newton_schulz_kernel, bf16((SEGMENT * rows, order)), [SMEM, VMEM, VM...  2.79 us
    pallas_call x1, Pallas kernels, on_device(): call(functools.partial(update_kernel, groups, 0.2 * math.sqrt(order)), [f...  2.4 us
  transfers between devices with their start and end apart: 1, of which 1 were waited for; matrix products, arithmetic and copies ran while one was open for 0% of the time, Pallas kernels for 0%

profile of v4, /device:TPU:1, one launch (start us, length us, event | category | flops | bytes accessed | tf_op | source)
XLA Modules:
  0.0 93.3 jit_solution(11292387159485309079)
XLA Ops:
  0.6 1.7 %fold_momentum.1 = (bf16[48,16,512]{2,1,0:T(8,128)(2,1)S(1)}, s32[64]{0:T(128)S(1)}) custom-call(s32[1]{0:T(128)} %bitcast.here_ref, s32[48]{0:T(128)} %owners_hbm.1, bf16[48,16,512]{2,1,0:T(8,128)(2,1)} %bitcast.6, f32[6,16,512]{2,1,0:T(8,128)} %momentum_ref.1), custom_call_target="tpu_custom_call" | custom-call | bytes 2097152 | tf_op jit(solution)/shard_map/fold_momentum/pallas_call | solution.py:275
  2.4 19.1 %all_to_all.20.parts_ref = bf16[16,3,16,512]{3,2,1,0:T(8,128)(2,1)S(1)} all-to-all(bf16[16,3,16,512]{3,2,1,0:T(8,128)(2,1)S(1)} %bitcast.8), channel_id=1, replica_groups=mesh['rep'=16,'fsdp'=32] {'rep'}, dimensions={0} | all-to-all | bytes 1572864 | tf_op jit(solution)/shard_map/reduce_over_rep/all_to_all | solution.py:290
  21.5 0.1 reduce_over_rep.1
  21.6 29.1 %all_to_all.21 = bf16[16,16,512]{2,1,0:T(8,128)(2,1)S(1)} all-to-all(bf16[16,16,512]{2,1,0:T(8,128)(2,1)S(1)} %get-tuple-element.9), channel_id=1, replica_groups={{0,2,4,6,8,10,12,14,16,18,20,22,24,26,28,30},{1,3,5,7,9,11,13,15,17,19,..., dimensions={0} | all-to-all | bytes 524288 | tf_op jit(solution)/shard_map/gather_rows/all_to_all | solution.py:300
  50.7 8.7 %collective-permute-start = (bf16[256,512]{1,0:T(8,128)(2,1)S(1)}, bf16[256,512]{1,0:T(8,128)(2,1)S(1)}, u32[]{:S(2)}, u32[]{:S(2)}) collective-permute-start(bf16[256,512]{1,0:T(8,128)(2,1)S(1)} %bitcast.9), channel_id=1, source_target_pairs={{0,1},{1,0},{2,3},{3,2},{4,5},{5,4},{6,7},{7,6},{8,9},{9,8},{10,11... | collective-permute-start | bytes 786440 | tf_op jit(solution)/shard_map/gather_rows/ppermute | solution.py:302
  59.5 1.1 %collective-permute-done.other_ref = bf16[256,512]{1,0:T(8,128)(2,1)S(1)} collective-permute-done((bf16[256,512]{1,0:T(8,128)(2,1)S(1)}, bf16[256,512]{1,0:T(8,128)(2,1)S(1)}, u32[]{:S(2)}, u32[]{:S(2)}) %collective-permute-start) | collective-permute-done | bytes 262176 | tf_op jit(solution)/shard_map/gather_rows/ppermute | solution.py:302
  60.6 2.8 %orthogonalize.1 = bf16[64,512]{1,0:T(8,128)(2,1)S(1)} custom-call(s32[1]{0:T(128)} %bitcast.2.segment_ref, bf16[256,512]{1,0:T(8,128)(2,1)S(1)} %bitcast.10, bf16[256,512]{1,0:T(8,128)(2,1)S(1)} %collective-permute-done.other_ref), custom_call_target="tpu_custom_call" | custom-call | flops 2013265920 | bytes 1048576 | tf_op jit(solution)/shard_map/orthogonalize/pallas_call | solution.py:305
  63.4 8.6 %all_to_all.22.returned_ref = bf16[4,16,512]{2,1,0:T(8,128)(2,1)S(1)} all-to-all(bf16[4,16,512]{2,1,0:T(8,128)(2,1)S(1)} %bitcast.11), channel_id=1, replica_groups={{0,2,4,6},{1,3,5,7},{8,10,12,14},{9,11,13,15},{16,18,20,22},{17,19,21,2..., dimensions={0} | all-to-all | bytes 131072 | tf_op jit(solution)/shard_map/return_rows/all_to_all | solution.py:314
  72.0 0.0 copy-start
  72.0 0.0 copy-start.1
  72.0 0.0 copy-start.2
  72.0 0.6 return_rows.1
  72.7 18.2 %all_to_all.23.both_ref = bf16[16,4,16,512]{3,2,1,0:T(8,128)(2,1)S(1)} all-to-all(bf16[16,4,16,512]{3,2,1,0:T(8,128)(2,1)S(1)} %return_rows.1), channel_id=1, replica_groups=mesh['rep'=16,'fsdp'=32] {'rep'}, dimensions={0} | all-to-all | bytes 2097152 | tf_op jit(solution)/shard_map/return_rows/all_to_all | solution.py:324
  90.9 0.0 copy-done
  90.9 0.0 copy-done.1
  90.9 0.0 copy-done.2
  90.9 2.4 %update.1 = (f32[48,16,512]{2,1,0:T(8,128)}, f32[48,16,512]{2,1,0:T(8,128)}, f32[6,16,512]{2,1,0:T(8,128)}) custom-call(s32[1]{0:T(128)} %bitcast.here_ref, s32[64]{0:T(128)S(1)} %get-tuple-element.7.ranks_any.ranks_ref, bf16[16,4,16,512]{3,2,1,0:T(8,128)(2,1)S(1)} %all_to_all.23.both_ref, f32[48,16,512]{2,1,0:T(8,128)S(1)} %copy-done.1, ...), custom_call_target="tpu_custom_call" | custom-call | bytes 5242880 | tf_op jit(solution)/shard_map/update/pallas_call | solution.py:326
Async XLA Ops:
  50.7 9.9 %collective-permute-start = (bf16[256,512]{1,0:T(8,128)(2,1)S(1)}, bf16[256,512]{1,0:T(8,128)(2,1)S(1)}, u32[]{:S(2)}, u32[]{:S(2)}) collective-permute-start(bf16[256,512]{1,0:T(8,128)(2,1)S(1)} %bitcast.9), channel_id=1, source_target_pairs={{0,1},{1,0},{2,3},{3,2},{4,5},{5,4},{6,7},{7,6},{8,9},{9,8},{10,11... | collective-permute-start | bytes 786440 | tf_op jit(solution)/shard_map/gather_rows/ppermute | solution.py:302
  72.0 18.8 %copy-start = (bf16[1,48,16,512]{3,2,1,0:T(8,128)(2,1)S(1)}, bf16[1,48,16,512]{3,2,1,0:T(8,128)(2,1)}, u32[]{:S(2)}) copy-start(bf16[1,48,16,512]{3,2,1,0:T(8,128)(2,1)} %param.4) | copy-start | bytes 2359300
  72.0 18.8 %copy-start.1 = (f32[48,16,512]{2,1,0:T(8,128)S(1)}, f32[48,16,512]{2,1,0:T(8,128)}, u32[]{:S(2)}) copy-start(f32[48,16,512]{2,1,0:T(8,128)} %weight_ref.1) | copy-start | bytes 4718596
  72.0 18.8 %copy-start.2 = (f32[6,16,512]{2,1,0:T(8,128)S(1)}, f32[6,16,512]{2,1,0:T(8,128)}, u32[]{:S(2)}) copy-start(f32[6,16,512]{2,1,0:T(8,128)} %momentum_ref.1) | copy-start | bytes 589828

commit v5 on v4

--- a/solution.py
+++ b/solution.py
@@ -19,6 +19,9 @@
 FOLD = MOMENTUM_DECAY * MOMENTUM_DECAY / DIRECTION_SCALE
 SEGMENT = 4
 PIECES = 6
+FIRST_GROUP = 14
+TOP_SEGMENTS = 3
+SEGMENT_ORDER = (2, 1, 3, 0)
 
 VMEM = pl.BlockSpec(memory_space=pltpu.VMEM)
 SMEM = pl.BlockSpec(memory_space=pltpu.SMEM)
@@ -96,7 +99,7 @@
 
     def target_of(block):
         group, place = split_rank(groups, ranks_ref[block])
-        return group * per_group + place
+        return ((group - FIRST_GROUP) & (groups - 1)) * per_group + place
 
     copies[1].wait()
     for block in range(blocks):
@@ -112,7 +115,7 @@
     ranks_out.wait()
 
 
-def sum_kernel(parts_ref, send_ref, total_ref):
+def sum_kernel(ring, parts_ref, send_ref, total_ref):
     count, blocks = parts_ref.shape[:2]
     for block in range(blocks):
         total = parts_ref[0, block].astype(jnp.float32)
@@ -120,8 +123,8 @@
             total = total + parts_ref[source, block].astype(jnp.float32)
         total_ref[block] = total.astype(jnp.bfloat16)
         direction = (DIRECTION_SCALE * total).astype(jnp.bfloat16)
-        for target in range(send_ref.shape[0]):
-            if min(target % SEGMENT, blocks - 1) == block:
+        for target, chip in enumerate(ring):
+            if min(chip % SEGMENT, blocks - 1) == block:
                 send_ref[target] = direction
 
 
@@ -133,7 +136,7 @@
     return jnp.dot(a, b, preferred_element_type=jnp.float32)
 
 
-def newton_schulz_kernel(segment_ref, own_ref, other_ref, out_ref, x_ref, y_ref, gram_ref, poly_ref):
+def newton_schulz_kernel(first_ref, own_ref, other_ref, out_ref, x_ref, y_ref, gram_ref, poly_ref):
     half, order = own_ref.shape
     kept = out_ref.shape[0]
     x_ref[0:half] = own_ref[...]
@@ -150,7 +153,7 @@
             gram = gram * (inverse * inverse)
         gram_ref[...] = gram.astype(jnp.bfloat16)
         last = iteration == NS_ITERS - 1
-        rows = pl.ds(pl.multiple_of(segment_ref[0] * kept, kept), kept) if last else pl.ds(0, order)
+        rows = pl.ds(pl.multiple_of(first_ref[0] * kept, kept), kept) if last else pl.ds(0, order)
         gram = gram_ref[rows]
         poly = (COEF_B * gram.astype(jnp.float32) + COEF_C * dot_nn(gram, gram_ref[...])).astype(jnp.bfloat16)
         if not last:
@@ -160,7 +163,10 @@
         if iteration == 0:
             fresh = fresh * inverse
         if last:
-            out_ref[...] = fresh.astype(jnp.bfloat16)
+            each = kept // SEGMENT
+            for target, chip in enumerate(SEGMENT_ORDER):
+                start = (SEGMENT - 1 - chip) * each
+                out_ref[target * each : (target + 1) * each] = fresh[start : start + each].astype(jnp.bfloat16)
         else:
             target_ref[...] = fresh.astype(jnp.bfloat16)
             source_ref, target_ref = target_ref, source_ref
@@ -172,7 +178,7 @@
     per_group = total_ref.shape[0]
     blocks = groups * per_group
     for place in range(per_group):
-        value = returned_ref[place]
+        value = returned_ref[SEGMENT_ORDER.index(place)]
         for target in range(groups):
             out_ref[target, place] = value
     value = total_ref[0]
@@ -263,13 +269,15 @@
     bf16 = functools.partial(jax.ShapeDtypeStruct, dtype=jnp.bfloat16)
     f32 = functools.partial(jax.ShapeDtypeStruct, dtype=jnp.float32)
     here = lax.axis_index("rep").astype(jnp.int32).reshape(1)
-    segment = (lax.axis_index("fsdp") // (2 * SEGMENT)).astype(jnp.int32).reshape(1)
-    same_core = [[2 * chip + core for chip in range(chips)] for core in range(2)]
+    segments = chips // SEGMENT
+    ring = [(SEGMENT * TOP_SEGMENTS - 1 - index) % chips for index in range(chips)]
+    same_core = [[2 * chip + core for chip in ring] for core in range(2)]
     same_segment = [
-        [2 * (SEGMENT * s + chip) + core for chip in range(SEGMENT)]
-        for s in range(chips // SEGMENT)
-        for core in range(2)
+        [2 * (SEGMENT * s + chip) + core for chip in SEGMENT_ORDER] for s in range(segments) for core in range(2)
     ]
+    from_first = [[(FIRST_GROUP + index) % groups for index in range(groups)]]
+    segment = lax.axis_index("fsdp") // (2 * SEGMENT)
+    listed = lax.rem(TOP_SEGMENTS - 1 + segments - segment, segments).astype(jnp.int32).reshape(1)
 
     with jax.named_scope("fold_momentum"):
         parts, ranks = call(
@@ -288,10 +296,15 @@
         )(here, *(pltpu.with_memory_space_constraint(array, pltpu.HBM) for array in (owners, part, momentum)))
     with jax.named_scope("reduce_over_rep"):
         received = lax.all_to_all(
-            parts.reshape(groups, per_group, rows, order), "rep", 0, 0, tiled=True
+            parts.reshape(groups, per_group, rows, order),
+            "rep",
+            0,
+            0,
+            axis_index_groups=from_first,
+            tiled=True,
         )
         send, total = call(
-            sum_kernel,
+            functools.partial(sum_kernel, ring),
             [bf16((chips, rows, order)), bf16((per_group, rows, order))],
             [VMEM],
             moved=1 << 20,
@@ -309,7 +322,7 @@
             [square] * 4,
             flops=15 * order**3,
             moved=1 << 20,
-        )(segment, own, other)
+        )(listed, own, other)
     with jax.named_scope("return_rows"):
         returned = lax.all_to_all(
             kept.reshape(SEGMENT, rows, order), "fsdp", 0, 0, axis_index_groups=same_segment, tiled=True

time: 94.2 us -> 87.9 us (0.933)
  starting transfers between devices: 8.73 us -> 4.46 us
  blocking collectives: 75.1 us -> 73.1 us
    ppermute x1, starting transfers between devices: 8.73 us -> 4.46 us  [on_device(): other = lax.ppermute(own, 'fsdp', [(i, i ^ 1) for i in range(members)])]
    all_to_all x1, blocking collectives: 19.1 us -> 15.1 us  [on_device(): lax.all_to_all(parts.reshape(groups, per_group, rows, order), 'rep', 0, 0...]
    all_to_all x1, blocking collectives: 8.64 us -> 5.96 us  [on_device(): lax.all_to_all(kept.reshape(SEGMENT, rows, order), 'fsdp', 0, 0, axis_ind...]
    all_to_all x1, blocking collectives: 18.2 us -> 20.9 us  [on_device(): both = lax.all_to_all(spread, 'rep', 0, 0, tiled=True)]
    all_to_all x1, blocking collectives: 29.1 us -> 31.2 us  [on_device(): lax.all_to_all(send, 'fsdp', 0, 0, axis_index_groups=same_core, tiled=True)]
where the time goes in v5:
time: 87.9 us; the launch traced here: 87 us
  blocking collectives  73.1 us (83%)
  Pallas kernels  7.64 us (9%)
  starting transfers between devices  4.46 us (5%)
  waiting for transfers between devices  1.12 us (1%)
    all_to_all x1, blocking collectives, on_device(): lax.all_to_all(send, 'fsdp', 0, 0, axis_index_groups=same_core, tiled=True)  31.2 us
    all_to_all x1, blocking collectives, on_device(): both = lax.all_to_all(spread, 'rep', 0, 0, tiled=True)  20.9 us
    all_to_all x1, blocking collectives, on_device(): lax.all_to_all(parts.reshape(groups, per_group, rows, order), 'rep', 0, 0...  15.1 us
    all_to_all x1, blocking collectives, on_device(): lax.all_to_all(kept.reshape(SEGMENT, rows, order), 'fsdp', 0, 0, axis_ind...  5.96 us
    ppermute x1, starting transfers between devices, on_device(): other = lax.ppermute(own, 'fsdp', [(i, i ^ 1) for i in range(members)])  4.46 us
    pallas_call x1, Pallas kernels, on_device(): call(newton_schulz_kernel, bf16((SEGMENT * rows, order)), [SMEM, VMEM, VM...  2.79 us
    pallas_call x1, Pallas kernels, on_device(): call(functools.partial(update_kernel, groups, 0.2 * math.sqrt(order)), [f...  2.4 us
  transfers between devices with their start and end apart: 1, of which 1 were waited for; matrix products, arithmetic and copies ran while one was open for 0% of the time, Pallas kernels for 0%

profile of v5, /device:TPU:1, one launch (start us, length us, event | category | flops | bytes accessed | tf_op | source)
XLA Modules:
  0.0 87.0 jit_solution(3251497948065355536)
XLA Ops:
  0.6 1.7 %fold_momentum.1 = (bf16[48,16,512]{2,1,0:T(8,128)(2,1)S(1)}, s32[64]{0:T(128)S(1)}) custom-call(s32[1]{0:T(128)} %bitcast.here_ref, s32[48]{0:T(128)} %owners_hbm.1, bf16[48,16,512]{2,1,0:T(8,128)(2,1)} %bitcast.6, f32[6,16,512]{2,1,0:T(8,128)} %momentum_ref.1), custom_call_target="tpu_custom_call" | custom-call | bytes 2097152 | tf_op jit(solution)/shard_map/fold_momentum/pallas_call | solution.py:283
  2.4 15.1 %all_to_all.20.parts_ref = bf16[16,3,16,512]{3,2,1,0:T(8,128)(2,1)S(1)} all-to-all(bf16[16,3,16,512]{3,2,1,0:T(8,128)(2,1)S(1)} %bitcast.8), channel_id=1, replica_groups={{448,480,0,32,64,96,128,160,192,224,256,288,320,352,384,416},{449,481,1..., dimensions={0} | all-to-all | bytes 1572864 | tf_op jit(solution)/shard_map/reduce_over_rep/all_to_all | solution.py:298
  17.4 0.1 reduce_over_rep.1
  17.5 31.2 %all_to_all.21 = bf16[16,16,512]{2,1,0:T(8,128)(2,1)S(1)} all-to-all(bf16[16,16,512]{2,1,0:T(8,128)(2,1)S(1)} %get-tuple-element.9), channel_id=1, replica_groups={{22,20,18,16,14,12,10,8,6,4,2,0,30,28,26,24},{23,21,19,17,15,13,11,9,7,..., dimensions={0} | all-to-all | bytes 524288 | tf_op jit(solution)/shard_map/gather_rows/all_to_all | solution.py:313
  48.8 4.5 %collective-permute-start = (bf16[256,512]{1,0:T(8,128)(2,1)S(1)}, bf16[256,512]{1,0:T(8,128)(2,1)S(1)}, u32[]{:S(2)}, u32[]{:S(2)}) collective-permute-start(bf16[256,512]{1,0:T(8,128)(2,1)S(1)} %bitcast.9), channel_id=1, source_target_pairs={{0,1},{1,0},{2,3},{3,2},{4,5},{5,4},{6,7},{7,6},{8,9},{9,8},{10,11... | collective-permute-start | bytes 786440 | tf_op jit(solution)/shard_map/gather_rows/ppermute | solution.py:315
  53.2 1.1 %collective-permute-done.other_ref = bf16[256,512]{1,0:T(8,128)(2,1)S(1)} collective-permute-done((bf16[256,512]{1,0:T(8,128)(2,1)S(1)}, bf16[256,512]{1,0:T(8,128)(2,1)S(1)}, u32[]{:S(2)}, u32[]{:S(2)}) %collective-permute-start) | collective-permute-done | bytes 262176 | tf_op jit(solution)/shard_map/gather_rows/ppermute | solution.py:315
  54.4 2.8 %orthogonalize.1 = bf16[64,512]{1,0:T(8,128)(2,1)S(1)} custom-call(s32[1]{0:T(128)} %bitcast.2.first_ref, bf16[256,512]{1,0:T(8,128)(2,1)S(1)} %bitcast.10, bf16[256,512]{1,0:T(8,128)(2,1)S(1)} %collective-permute-done.other_ref), custom_call_target="tpu_custom_call" | custom-call | flops 2013265920 | bytes 1048576 | tf_op jit(solution)/shard_map/orthogonalize/pallas_call | solution.py:318
  57.2 6.0 %all_to_all.22.returned_ref = bf16[4,16,512]{2,1,0:T(8,128)(2,1)S(1)} all-to-all(bf16[4,16,512]{2,1,0:T(8,128)(2,1)S(1)} %bitcast.11), channel_id=1, replica_groups={{4,2,6,0},{5,3,7,1},{12,10,14,8},{13,11,15,9},{20,18,22,16},{21,19,23,1..., dimensions={0} | all-to-all | bytes 131072 | tf_op jit(solution)/shard_map/return_rows/all_to_all | solution.py:327
  63.1 0.0 copy-start
  63.1 0.0 copy-start.1
  63.1 0.0 copy-start.2
  63.1 0.6 return_rows.1
  63.8 20.9 %all_to_all.23.both_ref = bf16[16,4,16,512]{3,2,1,0:T(8,128)(2,1)S(1)} all-to-all(bf16[16,4,16,512]{3,2,1,0:T(8,128)(2,1)S(1)} %return_rows.1), channel_id=1, replica_groups=mesh['rep'=16,'fsdp'=32] {'rep'}, dimensions={0} | all-to-all | bytes 2097152 | tf_op jit(solution)/shard_map/return_rows/all_to_all | solution.py:337
  84.6 0.0 copy-done
  84.6 0.0 copy-done.1
  84.6 0.0 copy-done.2
  84.6 2.4 %update.1 = (f32[48,16,512]{2,1,0:T(8,128)}, f32[48,16,512]{2,1,0:T(8,128)}, f32[6,16,512]{2,1,0:T(8,128)}) custom-call(s32[1]{0:T(128)} %bitcast.here_ref, s32[64]{0:T(128)S(1)} %get-tuple-element.7.ranks_any.ranks_ref, bf16[16,4,16,512]{3,2,1,0:T(8,128)(2,1)S(1)} %all_to_all.23.both_ref, f32[48,16,512]{2,1,0:T(8,128)S(1)} %copy-done.1, ...), custom_call_target="tpu_custom_call" | custom-call | bytes 5242880 | tf_op jit(solution)/shard_map/update/pallas_call | solution.py:339
Async XLA Ops:
  48.8 5.6 %collective-permute-start = (bf16[256,512]{1,0:T(8,128)(2,1)S(1)}, bf16[256,512]{1,0:T(8,128)(2,1)S(1)}, u32[]{:S(2)}, u32[]{:S(2)}) collective-permute-start(bf16[256,512]{1,0:T(8,128)(2,1)S(1)} %bitcast.9), channel_id=1, source_target_pairs={{0,1},{1,0},{2,3},{3,2},{4,5},{5,4},{6,7},{7,6},{8,9},{9,8},{10,11... | collective-permute-start | bytes 786440 | tf_op jit(solution)/shard_map/gather_rows/ppermute | solution.py:315
  63.1 21.5 %copy-start = (bf16[1,48,16,512]{3,2,1,0:T(8,128)(2,1)S(1)}, bf16[1,48,16,512]{3,2,1,0:T(8,128)(2,1)}, u32[]{:S(2)}) copy-start(bf16[1,48,16,512]{3,2,1,0:T(8,128)(2,1)} %param.4) | copy-start | bytes 2359300
  63.1 21.5 %copy-start.1 = (f32[48,16,512]{2,1,0:T(8,128)S(1)}, f32[48,16,512]{2,1,0:T(8,128)}, u32[]{:S(2)}) copy-start(f32[48,16,512]{2,1,0:T(8,128)} %weight_ref.1) | copy-start | bytes 4718596
  63.1 21.5 %copy-start.2 = (f32[6,16,512]{2,1,0:T(8,128)S(1)}, f32[6,16,512]{2,1,0:T(8,128)}, u32[]{:S(2)}) copy-start(f32[6,16,512]{2,1,0:T(8,128)} %momentum_ref.1) | copy-start | bytes 589828

commit v6 on v5

--- a/solution.py
+++ b/solution.py
@@ -26,7 +26,6 @@
 VMEM = pl.BlockSpec(memory_space=pltpu.VMEM)
 SMEM = pl.BlockSpec(memory_space=pltpu.SMEM)
 HBM = pl.BlockSpec(memory_space=pltpu.HBM)
-ANY = pl.BlockSpec(memory_space=pl.ANY)
 
 
 def folded(part, momentum):
@@ -73,7 +72,6 @@
     part_hbm,
     momentum_hbm,
     out_ref,
-    ranks_out_ref,
     owners_ref,
     ranks_ref,
     owned_ref,
@@ -93,8 +91,6 @@
         copy.start()
     copies[0].wait()
     rank_blocks(groups, owners_ref, ranks_ref)
-    ranks_out = pltpu.make_async_copy(ranks_ref, ranks_out_ref, sems.at[3])
-    ranks_out.start()
     _, count = list_owned(blocks, groups, here_ref[0], ranks_ref, owned_ref)
 
     def target_of(block):
@@ -112,7 +108,23 @@
             block = owned_ref[slot]
             out_ref[target_of(block)] = folded(part_ref[block], momentum_ref[slot])
 
-    ranks_out.wait()
+
+def sums_kernel(groups, here_ref, owners_ref, total_ref, out_ref, ranks_out_ref, ranks_ref, sem):
+    rank_blocks(groups, owners_ref, ranks_ref)
+    copy = pltpu.make_async_copy(ranks_ref, ranks_out_ref, sem)
+    copy.start()
+    per_group = total_ref.shape[0]
+    blocks = groups * per_group
+    value = total_ref[0]
+    for target in range(groups):
+        out_ref[target, per_group] = value
+    for place in range(per_group):
+        rank = place * groups + here_ref[0]
+        owner = jnp.int32(-1)
+        for group in range(groups):
+            owner = owner + (ranks_ref[blocks + group] <= rank).astype(jnp.int32)
+        out_ref[owner, per_group] = total_ref[place]
+    copy.wait()
 
 
 def sum_kernel(ring, parts_ref, send_ref, total_ref):
@@ -172,25 +184,12 @@
             source_ref, target_ref = target_ref, source_ref
 
 
-def spread_kernel(groups, here_ref, ranks_any, returned_ref, total_ref, out_ref, ranks_ref, sem):
-    copy = pltpu.make_async_copy(ranks_any, ranks_ref, sem)
-    copy.start()
-    per_group = total_ref.shape[0]
-    blocks = groups * per_group
-    for place in range(per_group):
+def spread_kernel(returned_ref, sums_ref, out_ref):
+    del sums_ref
+    for place in range(out_ref.shape[1] - 1):
         value = returned_ref[SEGMENT_ORDER.index(place)]
-        for target in range(groups):
+        for target in range(out_ref.shape[0]):
             out_ref[target, place] = value
-    value = total_ref[0]
-    for target in range(groups):
-        out_ref[target, per_group] = value
-    copy.wait()
-    for place in range(per_group):
-        rank = place * groups + here_ref[0]
-        owner = jnp.int32(-1)
-        for group in range(groups):
-            owner = owner + (ranks_ref[blocks + group] <= rank).astype(jnp.int32)
-        out_ref[owner, per_group] = total_ref[place]
 
 
 def update_kernel(
@@ -245,13 +244,14 @@
         copy.wait()
 
 
-def call(kernel, out_shape, in_specs, scratch=(), flops=0, moved=0, out_specs=None, room=40.0):
+def call(kernel, out_shape, in_specs, scratch=(), flops=0, moved=0, out_specs=None, room=40.0, aliases={}):
     return pl.pallas_call(
         kernel,
         out_shape=out_shape,
         in_specs=in_specs,
         out_specs=jax.tree.map(lambda _: VMEM, out_shape) if out_specs is None else out_specs,
         scratch_shapes=list(scratch),
+        input_output_aliases=aliases,
         compiler_params=pltpu.CompilerParams(vmem_limit_bytes=int((64 - room) * 1024 * 1024)),
         cost_estimate=pl.CostEstimate(flops=flops, bytes_accessed=moved, transcendentals=0),
     )
@@ -280,9 +280,9 @@
     listed = lax.rem(TOP_SEGMENTS - 1 + segments - segment, segments).astype(jnp.int32).reshape(1)
 
     with jax.named_scope("fold_momentum"):
-        parts, ranks = call(
+        parts = call(
             functools.partial(fold_kernel, groups),
-            [pltpu.VMEM((blocks, rows, order), jnp.bfloat16), pltpu.VMEM((ranks_size,), jnp.int32)],
+            pltpu.VMEM((blocks, rows, order), jnp.bfloat16),
             [SMEM, HBM, HBM, HBM],
             [
                 pltpu.SMEM((blocks,), jnp.int32),
@@ -290,7 +290,7 @@
                 pltpu.SMEM((most + 1,), jnp.int32),
                 pltpu.VMEM(part.shape, jnp.bfloat16),
                 pltpu.VMEM(momentum.shape, jnp.float32),
-                pltpu.SemaphoreType.DMA((4,)),
+                pltpu.SemaphoreType.DMA((3,)),
             ],
             moved=1 << 21,
         )(here, *(pltpu.with_memory_space_constraint(array, pltpu.HBM) for array in (owners, part, momentum)))
@@ -313,6 +313,19 @@
         own = lax.all_to_all(send, "fsdp", 0, 0, axis_index_groups=same_core, tiled=True)
         own = own.reshape(chips * rows, order)
         other = lax.ppermute(own, "fsdp", [(i, i ^ 1) for i in range(members)])
+    with jax.named_scope("sums_to_owners"):
+        late_owners, own = lax.optimization_barrier((owners, own))
+        sums, ranks = call(
+            functools.partial(sums_kernel, groups),
+            [
+                pltpu.VMEM((groups, per_group + 1, rows, order), jnp.bfloat16),
+                pltpu.VMEM((ranks_size,), jnp.int32),
+            ],
+            [SMEM, SMEM, VMEM],
+            [pltpu.SMEM((ranks_size,), jnp.int32), pltpu.SemaphoreType.DMA],
+            moved=1 << 20,
+        )(here, late_owners, total)
+        other, ranks = lax.optimization_barrier((other, ranks))
     with jax.named_scope("orthogonalize"):
         square = pltpu.VMEM((order, order), jnp.bfloat16)
         kept = call(
@@ -328,12 +341,12 @@
             kept.reshape(SEGMENT, rows, order), "fsdp", 0, 0, axis_index_groups=same_segment, tiled=True
         )
         spread = call(
-            functools.partial(spread_kernel, groups),
-            bf16((groups, per_group + 1, rows, order)),
-            [SMEM, ANY, VMEM, VMEM],
-            [pltpu.SMEM((ranks_size,), jnp.int32), pltpu.SemaphoreType.DMA],
+            spread_kernel,
+            bf16(sums.shape),
+            [VMEM, VMEM],
             moved=1 << 20,
-        )(here, ranks, returned, total)
+            aliases={1: 0},
+        )(returned, sums)
         both = lax.all_to_all(spread, "rep", 0, 0, tiled=True)
     with jax.named_scope("update"):
         return call(

time: 87.9 us -> 87.6 us (level)
  waiting for transfers between devices: 1.12 us -> 0.01 us
    ppermute x1, waiting for transfers between devices: 1.12 us -> 0.01 us  [on_device(): other = lax.ppermute(own, 'fsdp', [(i, i ^ 1) for i in range(members)])]
    pallas_call x2 -> x3, Pallas kernels: 2.34 us -> 3.09 us  [the longest x1 1.61 us: on_device(): call(functools.partial(sums_kernel, groups), [pltpu.VMEM((groups, per_gro...]
  transfers between devices with their start and end apart: 1 -> 1, of which waited for: 1 -> 0; matrix products, arithmetic and copies ran while one was open for 0% -> 0% of each run, Pallas kernels for 0% -> 2%
where the time goes in v6:
time: 87.6 us; the launch traced here: 86.4 us
  blocking collectives  72.8 us (83%)
  Pallas kernels  8.4 us (10%)
  starting transfers between devices  4.46 us (5%)
    all_to_all x1, blocking collectives, on_device(): lax.all_to_all(send, 'fsdp', 0, 0, axis_index_groups=same_core, tiled=True)  31.2 us
    all_to_all x1, blocking collectives, on_device(): both = lax.all_to_all(spread, 'rep', 0, 0, tiled=True)  20.5 us
    all_to_all x1, blocking collectives, on_device(): lax.all_to_all(parts.reshape(groups, per_group, rows, order), 'rep', 0, 0...  15.1 us
    all_to_all x1, blocking collectives, on_device(): lax.all_to_all(kept.reshape(SEGMENT, rows, order), 'fsdp', 0, 0, axis_ind...  5.97 us
    ppermute x1, starting transfers between devices, on_device(): other = lax.ppermute(own, 'fsdp', [(i, i ^ 1) for i in range(members)])  4.46 us
    pallas_call x1, Pallas kernels, on_device(): call(newton_schulz_kernel, bf16((SEGMENT * rows, order)), [SMEM, VMEM, VM...  2.79 us
    pallas_call x1, Pallas kernels, on_device(): call(functools.partial(update_kernel, groups, 0.2 * math.sqrt(order)), [f...  2.4 us
  transfers between devices with their start and end apart: 1, of which 0 were waited for; matrix products, arithmetic and copies ran while one was open for 0% of the time, Pallas kernels for 2%

profile of v6, /device:TPU:1, one launch (start us, length us, event | category | flops | bytes accessed | tf_op | source)
XLA Modules:
  0.0 86.4 jit_solution(16876804354148368134)
XLA Ops:
  0.6 1.4 %fold_momentum.1 = bf16[48,16,512]{2,1,0:T(8,128)(2,1)S(1)} custom-call(s32[1]{0:T(128)} %bitcast.here_ref, s32[48]{0:T(128)} %owners_ref, bf16[48,16,512]{2,1,0:T(8,128)(2,1)} %bitcast.7, f32[6,16,512]{2,1,0:T(8,128)} %momentum_ref.1), custom_call_target="tpu_custom_call" | custom-call | bytes 2097152 | tf_op jit(solution)/shard_map/fold_momentum/pallas_call | solution.py:283
  2.1 0.0 copy-start.3
  2.1 15.1 %all_to_all.20.parts_ref = bf16[16,3,16,512]{3,2,1,0:T(8,128)(2,1)S(1)} all-to-all(bf16[16,3,16,512]{3,2,1,0:T(8,128)(2,1)S(1)} %bitcast.6), channel_id=1, replica_groups={{448,480,0,32,64,96,128,160,192,224,256,288,320,352,384,416},{449,481,1..., dimensions={0} | all-to-all | bytes 1572864 | tf_op jit(solution)/shard_map/reduce_over_rep/all_to_all | solution.py:298
  17.1 0.1 reduce_over_rep.1
  17.3 31.2 %all_to_all.21 = bf16[16,16,512]{2,1,0:T(8,128)(2,1)S(1)} all-to-all(bf16[16,16,512]{2,1,0:T(8,128)(2,1)S(1)} %get-tuple-element.11), channel_id=1, replica_groups={{22,20,18,16,14,12,10,8,6,4,2,0,30,28,26,24},{23,21,19,17,15,13,11,9,7,..., dimensions={0} | all-to-all | bytes 524288 | tf_op jit(solution)/shard_map/gather_rows/all_to_all | solution.py:313
  48.5 4.5 %collective-permute-start = (bf16[256,512]{1,0:T(8,128)(2,1)S(1)}, bf16[256,512]{1,0:T(8,128)(2,1)S(1)}, u32[]{:S(2)}, u32[]{:S(2)}) collective-permute-start(bf16[256,512]{1,0:T(8,128)(2,1)S(1)} %bitcast.9), channel_id=1, source_target_pairs={{0,1},{1,0},{2,3},{3,2},{4,5},{5,4},{6,7},{7,6},{8,9},{9,8},{10,11... | collective-permute-start | bytes 786440 | tf_op jit(solution)/shard_map/gather_rows/ppermute | solution.py:315
  53.0 0.0 copy-done.3
  53.0 1.6 %sums_to_owners.1 = (bf16[16,4,16,512]{3,2,1,0:T(8,128)(2,1)S(1)}, s32[64]{0:T(128)S(1)}) custom-call(s32[1]{0:T(128)} %bitcast.here_ref, s32[48]{0:T(128)S(1)} %copy-done.3, bf16[3,16,512]{2,1,0:T(8,128)(2,1)S(1)} %get-tuple-element.13.total_ref), custom_call_target="tpu_custom_call" | custom-call | bytes 1048576 | tf_op jit(solution)/shard_map/sums_to_owners/pallas_call | solution.py:318
  54.6 0.0 collective-permute-done.other_ref
  54.6 2.8 %orthogonalize.1 = bf16[64,512]{1,0:T(8,128)(2,1)S(1)} custom-call(s32[1]{0:T(128)} %bitcast.4.first_ref, bf16[256,512]{1,0:T(8,128)(2,1)S(1)} %bitcast.10, bf16[256,512]{1,0:T(8,128)(2,1)S(1)} %collective-permute-done.other_ref), custom_call_target="tpu_custom_call" | custom-call | flops 2013265920 | bytes 1048576 | tf_op jit(solution)/shard_map/orthogonalize/pallas_call | solution.py:331
  57.4 6.0 %all_to_all.22.returned_ref = bf16[4,16,512]{2,1,0:T(8,128)(2,1)S(1)} all-to-all(bf16[4,16,512]{2,1,0:T(8,128)(2,1)S(1)} %bitcast.11), channel_id=1, replica_groups={{4,2,6,0},{5,3,7,1},{12,10,14,8},{13,11,15,9},{20,18,22,16},{21,19,23,1..., dimensions={0} | all-to-all | bytes 131072 | tf_op jit(solution)/shard_map/return_rows/all_to_all | solution.py:340
  63.4 0.0 copy-start.1
  63.4 0.1 return_rows.1
  63.4 0.0 copy-start
  63.5 0.0 copy-start.2
  63.5 20.5 %all_to_all.23.both_ref = bf16[16,4,16,512]{3,2,1,0:T(8,128)(2,1)S(1)} all-to-all(bf16[16,4,16,512]{3,2,1,0:T(8,128)(2,1)S(1)} %return_rows.1), channel_id=1, replica_groups=mesh['rep'=16,'fsdp'=32] {'rep'}, dimensions={0} | all-to-all | bytes 2097152 | tf_op jit(solution)/shard_map/return_rows/all_to_all | solution.py:350
  84.0 0.0 copy-done.1
  84.0 0.0 copy-done
  84.0 0.0 copy-done.2
  84.0 2.4 %update.1 = (f32[48,16,512]{2,1,0:T(8,128)}, f32[48,16,512]{2,1,0:T(8,128)}, f32[6,16,512]{2,1,0:T(8,128)}) custom-call(s32[1]{0:T(128)} %bitcast.here_ref, s32[64]{0:T(128)S(1)} %get-tuple-element.15.ranks_ref, bf16[16,4,16,512]{3,2,1,0:T(8,128)(2,1)S(1)} %all_to_all.23.both_ref, f32[48,16,512]{2,1,0:T(8,128)S(1)} %copy-done.1, ...), custom_call_target="tpu_custom_call" | custom-call | bytes 5242880 | tf_op jit(solution)/shard_map/update/pallas_call | solution.py:352
Async XLA Ops:
  2.1 50.9 %copy-start.3 = (s32[48]{0:T(128)S(1)}, s32[48]{0:T(128)}, u32[]{:S(2)}) copy-start(s32[48]{0:T(128)} %owners_ref) | copy-start | bytes 580
  48.5 6.1 %collective-permute-start = (bf16[256,512]{1,0:T(8,128)(2,1)S(1)}, bf16[256,512]{1,0:T(8,128)(2,1)S(1)}, u32[]{:S(2)}, u32[]{:S(2)}) collective-permute-start(bf16[256,512]{1,0:T(8,128)(2,1)S(1)} %bitcast.9), channel_id=1, source_target_pairs={{0,1},{1,0},{2,3},{3,2},{4,5},{5,4},{6,7},{7,6},{8,9},{9,8},{10,11... | collective-permute-start | bytes 786440 | tf_op jit(solution)/shard_map/gather_rows/ppermute | solution.py:315
  63.4 20.7 %copy-start.1 = (f32[48,16,512]{2,1,0:T(8,128)S(1)}, f32[48,16,512]{2,1,0:T(8,128)}, u32[]{:S(2)}) copy-start(f32[48,16,512]{2,1,0:T(8,128)} %weight_ref.1) | copy-start | bytes 4718596
  63.4 20.6 %copy-start = (bf16[1,48,16,512]{3,2,1,0:T(8,128)(2,1)S(1)}, bf16[1,48,16,512]{3,2,1,0:T(8,128)(2,1)}, u32[]{:S(2)}) copy-start(bf16[1,48,16,512]{3,2,1,0:T(8,128)(2,1)} %param.4) | copy-start | bytes 2359300
  63.5 20.6 %copy-start.2 = (f32[6,16,512]{2,1,0:T(8,128)S(1)}, f32[6,16,512]{2,1,0:T(8,128)}, u32[]{:S(2)}) copy-start(f32[6,16,512]{2,1,0:T(8,128)} %momentum_ref.1) | copy-start | bytes 589828

commit v7 on v6

--- a/solution.py
+++ b/solution.py
@@ -32,37 +32,24 @@
     return (part.astype(jnp.float32) + FOLD * momentum).astype(jnp.bfloat16)
 
 
-def rank_blocks(groups, owners_ref, ranks_ref):
-    blocks = owners_ref.shape[0]
+def count_slots(owners_ref, first_ref, rank_ref):
+    groups = first_ref.shape[0]
     for group in range(groups):
-        ranks_ref[blocks + group] = 0
-    for block in range(blocks):
+        first_ref[group] = 0
+    for block in range(owners_ref.shape[0]):
         owner = owners_ref[block]
-        slot = ranks_ref[blocks + owner]
-        ranks_ref[block] = slot
-        ranks_ref[blocks + owner] = slot + 1
+        slot = first_ref[owner]
+        rank_ref[block] = slot
+        first_ref[owner] = slot + 1
     first = jnp.int32(0)
     for group in range(groups):
-        after = first + ranks_ref[blocks + group]
-        ranks_ref[blocks + group] = first
+        after = first + first_ref[group]
+        first_ref[group] = first
         first = after
-    for block in range(blocks):
-        ranks_ref[block] = ranks_ref[blocks + owners_ref[block]] + ranks_ref[block]
 
 
 def split_rank(groups, rank):
     return rank & (groups - 1), rank >> (groups.bit_length() - 1)
-
-
-def list_owned(blocks, groups, here, ranks_ref, owned_ref):
-    first = ranks_ref[blocks + here]
-    after = jnp.where(here == groups - 1, blocks, ranks_ref[blocks + jnp.minimum(here + 1, groups - 1)])
-    count = after - first
-    unused = owned_ref.shape[0] - 1
-    for block in range(blocks):
-        slot = ranks_ref[block] - first
-        owned_ref[jnp.where((slot >= 0) & (slot < count), slot, unused)] = block
-    return first, count
 
 
 def fold_kernel(
@@ -73,7 +60,8 @@
     momentum_hbm,
     out_ref,
     owners_ref,
-    ranks_ref,
+    first_ref,
+    target_ref,
     owned_ref,
     part_ref,
     momentum_ref,
@@ -89,32 +77,42 @@
     ]
     for copy in copies:
         copy.start()
+    here = here_ref[0]
     copies[0].wait()
-    rank_blocks(groups, owners_ref, ranks_ref)
-    _, count = list_owned(blocks, groups, here_ref[0], ranks_ref, owned_ref)
-
-    def target_of(block):
-        group, place = split_rank(groups, ranks_ref[block])
-        return ((group - FIRST_GROUP) & (groups - 1)) * per_group + place
-
+    count_slots(owners_ref, first_ref, target_ref)
+    count = jnp.int32(0)
+    for block in range(blocks):
+        owner, slot = owners_ref[block], target_ref[block]
+        mine = owner == here
+        count = count + mine.astype(jnp.int32)
+        owned_ref[jnp.where(mine, slot, most)] = block
+        group, place = split_rank(groups, first_ref[owner] + slot)
+        target_ref[block] = ((group - FIRST_GROUP) & (groups - 1)) * per_group + place
     copies[1].wait()
     for block in range(blocks):
-        out_ref[target_of(block)] = part_ref[block]
+        out_ref[target_ref[block]] = part_ref[block]
     copies[2].wait()
     for slot in range(most):
 
         @pl.when(slot < count)
         def _():
             block = owned_ref[slot]
-            out_ref[target_of(block)] = folded(part_ref[block], momentum_ref[slot])
-
-
-def sums_kernel(groups, here_ref, owners_ref, total_ref, out_ref, ranks_out_ref, ranks_ref, sem):
-    rank_blocks(groups, owners_ref, ranks_ref)
-    copy = pltpu.make_async_copy(ranks_ref, ranks_out_ref, sem)
-    copy.start()
+            out_ref[target_ref[block]] = folded(part_ref[block], momentum_ref[slot])
+
+
+def sums_kernel(
+    groups, here_ref, owners_ref, total_ref, out_ref, first_out_ref, rank_out_ref, first_ref, rank_ref, sems
+):
     per_group = total_ref.shape[0]
-    blocks = groups * per_group
+    count_slots(owners_ref, first_ref, rank_ref)
+    for block in range(owners_ref.shape[0]):
+        rank_ref[block] = first_ref[owners_ref[block]] + rank_ref[block]
+    copies = [
+        pltpu.make_async_copy(source, target, sems.at[index])
+        for index, (source, target) in enumerate([(first_ref, first_out_ref), (rank_ref, rank_out_ref)])
+    ]
+    for copy in copies:
+        copy.start()
     value = total_ref[0]
     for target in range(groups):
         out_ref[target, per_group] = value
@@ -122,9 +120,10 @@
         rank = place * groups + here_ref[0]
         owner = jnp.int32(-1)
         for group in range(groups):
-            owner = owner + (ranks_ref[blocks + group] <= rank).astype(jnp.int32)
+            owner = owner + (first_ref[group] <= rank).astype(jnp.int32)
         out_ref[owner, per_group] = total_ref[place]
-    copy.wait()
+    for copy in copies:
+        copy.wait()
 
 
 def sum_kernel(ring, parts_ref, send_ref, total_ref):
@@ -196,7 +195,8 @@
     groups,
     scale,
     here_ref,
-    ranks_ref,
+    first_ref,
+    rank_ref,
     both_ref,
     weight_ref,
     part_ref,
@@ -223,13 +223,19 @@
     for index in range(PIECES):
         chunk = pl.ds(index * each, each)
         for block in range(index * each, (index + 1) * each):
-            group, place = split_rank(groups, ranks_ref[block])
+            group, place = split_rank(groups, rank_ref[block])
             step = both_ref[group, place].astype(jnp.float32) * scale
             step_ref[block] = step
             new_ref[block] = weight_ref[block] - LEARN_RATE * step
         leave(step_ref.at[chunk], step_hbm.at[chunk], sems.at[index, 0])
         leave(new_ref.at[chunk], new_hbm.at[chunk], sems.at[index, 1])
-    first, count = list_owned(blocks, groups, here_ref[0], ranks_ref, owned_ref)
+    here = here_ref[0]
+    first = first_ref[here]
+    after = jnp.where(here == groups - 1, blocks, first_ref[jnp.minimum(here + 1, groups - 1)])
+    count = after - first
+    for block in range(blocks):
+        slot = rank_ref[block] - first
+        owned_ref[jnp.where((slot >= 0) & (slot < count), slot, most)] = block
     for slot in range(most):
         used = slot < count
         block = jnp.where(used, owned_ref[slot], 0)
@@ -265,7 +271,6 @@
     members = lax.axis_size("fsdp")
     chips = members // 2
     per_group = blocks // groups
-    ranks_size = blocks + groups
     bf16 = functools.partial(jax.ShapeDtypeStruct, dtype=jnp.bfloat16)
     f32 = functools.partial(jax.ShapeDtypeStruct, dtype=jnp.float32)
     here = lax.axis_index("rep").astype(jnp.int32).reshape(1)
@@ -286,7 +291,8 @@
             [SMEM, HBM, HBM, HBM],
             [
                 pltpu.SMEM((blocks,), jnp.int32),
-                pltpu.SMEM((ranks_size,), jnp.int32),
+                pltpu.SMEM((groups,), jnp.int32),
+                pltpu.SMEM((blocks,), jnp.int32),
                 pltpu.SMEM((most + 1,), jnp.int32),
                 pltpu.VMEM(part.shape, jnp.bfloat16),
                 pltpu.VMEM(momentum.shape, jnp.float32),
@@ -315,14 +321,19 @@
         other = lax.ppermute(own, "fsdp", [(i, i ^ 1) for i in range(members)])
     with jax.named_scope("sums_to_owners"):
         late_owners, own = lax.optimization_barrier((owners, own))
-        sums, ranks = call(
+        sums, first, ranks = call(
             functools.partial(sums_kernel, groups),
             [
                 pltpu.VMEM((groups, per_group + 1, rows, order), jnp.bfloat16),
-                pltpu.VMEM((ranks_size,), jnp.int32),
+                pltpu.VMEM((groups,), jnp.int32),
+                pltpu.VMEM((blocks,), jnp.int32),
             ],
             [SMEM, SMEM, VMEM],
-            [pltpu.SMEM((ranks_size,), jnp.int32), pltpu.SemaphoreType.DMA],
+            [
+                pltpu.SMEM((groups,), jnp.int32),
+                pltpu.SMEM((blocks,), jnp.int32),
+                pltpu.SemaphoreType.DMA((2,)),
+            ],
             moved=1 << 20,
         )(here, late_owners, total)
         other, ranks = lax.optimization_barrier((other, ranks))
@@ -352,7 +363,7 @@
         return call(
             functools.partial(update_kernel, groups, 0.2 * math.sqrt(order)),
             [f32(weight.shape), f32(weight.shape), f32(momentum.shape)],
-            [SMEM, SMEM, VMEM, VMEM, VMEM, VMEM],
+            [SMEM, SMEM, SMEM, VMEM, VMEM, VMEM, VMEM],
             [
                 pltpu.SMEM((most + 1,), jnp.int32),
                 pltpu.VMEM(weight.shape, jnp.float32),
@@ -363,7 +374,7 @@
             ],
             moved=5 << 20,
             out_specs=[HBM, HBM, HBM],
-        )(here, ranks, both, weight, part, momentum)
+        )(here, first, ranks, both, weight, part, momentum)
 
 
 def solution(mesh):

time: 87.6 us -> 87.3 us (level)
  no operation moved by 1% of the time
where the time goes in v7:
time: 87.3 us; the launch traced here: 86.2 us
  blocking collectives  72.8 us (83%)
  Pallas kernels  8.16 us (9%)
  starting transfers between devices  4.46 us (5%)
    all_to_all x1, blocking collectives, on_device(): lax.all_to_all(send, 'fsdp', 0, 0, axis_index_groups=same_core, tiled=True)  31.2 us
    all_to_all x1, blocking collectives, on_device(): both = lax.all_to_all(spread, 'rep', 0, 0, tiled=True)  20.5 us
    all_to_all x1, blocking collectives, on_device(): lax.all_to_all(parts.reshape(groups, per_group, rows, order), 'rep', 0, 0...  15.1 us
    all_to_all x1, blocking collectives, on_device(): lax.all_to_all(kept.reshape(SEGMENT, rows, order), 'fsdp', 0, 0, axis_ind...  5.96 us
    ppermute x1, starting transfers between devices, on_device(): other = lax.ppermute(own, 'fsdp', [(i, i ^ 1) for i in range(members)])  4.46 us
    pallas_call x1, Pallas kernels, on_device(): call(newton_schulz_kernel, bf16((SEGMENT * rows, order)), [SMEM, VMEM, VM...  2.8 us
    pallas_call x1, Pallas kernels, on_device(): call(functools.partial(update_kernel, groups, 0.2 * math.sqrt(order)), [f...  2.4 us
  transfers between devices with their start and end apart: 1, of which 0 were waited for; matrix products, arithmetic and copies ran while one was open for 0% of the time, Pallas kernels for 2%

profile of v7, /device:TPU:1, one launch (start us, length us, event | category | flops | bytes accessed | tf_op | source)
XLA Modules:
  0.0 86.2 jit_solution(11771716515013419327)
XLA Ops:
  0.6 1.3 %fold_momentum.1 = bf16[48,16,512]{2,1,0:T(8,128)(2,1)S(1)} custom-call(s32[1]{0:T(128)} %bitcast.here_ref, s32[48]{0:T(128)} %owners_ref, bf16[48,16,512]{2,1,0:T(8,128)(2,1)} %bitcast.7, f32[6,16,512]{2,1,0:T(8,128)} %momentum_ref.1), custom_call_target="tpu_custom_call" | custom-call | bytes 2097152 | tf_op jit(solution)/shard_map/fold_momentum/pallas_call | solution.py:288
  1.9 0.0 copy-start.3
  1.9 15.1 %all_to_all.20.parts_ref = bf16[16,3,16,512]{3,2,1,0:T(8,128)(2,1)S(1)} all-to-all(bf16[16,3,16,512]{3,2,1,0:T(8,128)(2,1)S(1)} %bitcast.6), channel_id=1, replica_groups={{448,480,0,32,64,96,128,160,192,224,256,288,320,352,384,416},{449,481,1..., dimensions={0} | all-to-all | bytes 1572864 | tf_op jit(solution)/shard_map/reduce_over_rep/all_to_all | solution.py:304
  17.0 0.1 reduce_over_rep.1
  17.1 31.2 %all_to_all.21 = bf16[16,16,512]{2,1,0:T(8,128)(2,1)S(1)} all-to-all(bf16[16,16,512]{2,1,0:T(8,128)(2,1)S(1)} %get-tuple-element.12), channel_id=1, replica_groups={{22,20,18,16,14,12,10,8,6,4,2,0,30,28,26,24},{23,21,19,17,15,13,11,9,7,..., dimensions={0} | all-to-all | bytes 524288 | tf_op jit(solution)/shard_map/gather_rows/all_to_all | solution.py:319
  48.3 4.5 %collective-permute-start = (bf16[256,512]{1,0:T(8,128)(2,1)S(1)}, bf16[256,512]{1,0:T(8,128)(2,1)S(1)}, u32[]{:S(2)}, u32[]{:S(2)}) collective-permute-start(bf16[256,512]{1,0:T(8,128)(2,1)S(1)} %bitcast.9), channel_id=1, source_target_pairs={{0,1},{1,0},{2,3},{3,2},{4,5},{5,4},{6,7},{7,6},{8,9},{9,8},{10,11... | collective-permute-start | bytes 786440 | tf_op jit(solution)/shard_map/gather_rows/ppermute | solution.py:321
  52.8 0.0 copy-done.3
  52.8 1.5 %sums_to_owners.1 = (bf16[16,4,16,512]{3,2,1,0:T(8,128)(2,1)S(1)}, s32[16]{0:T(128)S(1)}, s32[48]{0:T(128)S(1)}) custom-call(s32[1]{0:T(128)} %bitcast.here_ref, s32[48]{0:T(128)S(1)} %copy-done.3, bf16[3,16,512]{2,1,0:T(8,128)(2,1)S(1)} %get-tuple-element.14.total_ref), custom_call_target="tpu_custom_call" | custom-call | bytes 1048576 | tf_op jit(solution)/shard_map/sums_to_owners/pallas_call | solution.py:324
  54.3 0.0 collective-permute-done.other_ref
  54.3 2.8 %orthogonalize.1 = bf16[64,512]{1,0:T(8,128)(2,1)S(1)} custom-call(s32[1]{0:T(128)} %bitcast.4.first_ref, bf16[256,512]{1,0:T(8,128)(2,1)S(1)} %bitcast.10, bf16[256,512]{1,0:T(8,128)(2,1)S(1)} %collective-permute-done.other_ref), custom_call_target="tpu_custom_call" | custom-call | flops 2013265920 | bytes 1048576 | tf_op jit(solution)/shard_map/orthogonalize/pallas_call | solution.py:342
  57.1 6.0 %all_to_all.22.returned_ref = bf16[4,16,512]{2,1,0:T(8,128)(2,1)S(1)} all-to-all(bf16[4,16,512]{2,1,0:T(8,128)(2,1)S(1)} %bitcast.11), channel_id=1, replica_groups={{4,2,6,0},{5,3,7,1},{12,10,14,8},{13,11,15,9},{20,18,22,16},{21,19,23,1..., dimensions={0} | all-to-all | bytes 131072 | tf_op jit(solution)/shard_map/return_rows/all_to_all | solution.py:351
  63.1 0.0 copy-start.1
  63.1 0.1 return_rows.1
  63.2 0.0 copy-start
  63.2 0.0 copy-start.2
  63.2 20.5 %all_to_all.23.both_ref = bf16[16,4,16,512]{3,2,1,0:T(8,128)(2,1)S(1)} all-to-all(bf16[16,4,16,512]{3,2,1,0:T(8,128)(2,1)S(1)} %return_rows.1), channel_id=1, replica_groups=mesh['rep'=16,'fsdp'=32] {'rep'}, dimensions={0} | all-to-all | bytes 2097152 | tf_op jit(solution)/shard_map/return_rows/all_to_all | solution.py:361
  83.7 0.0 copy-done.1
  83.7 0.0 copy-done
  83.7 0.0 copy-done.2
  83.8 2.4 %update.1 = (f32[48,16,512]{2,1,0:T(8,128)}, f32[48,16,512]{2,1,0:T(8,128)}, f32[6,16,512]{2,1,0:T(8,128)}) custom-call(s32[1]{0:T(128)} %bitcast.here_ref, s32[16]{0:T(128)S(1)} %get-tuple-element.15.first_ref, s32[48]{0:T(128)S(1)} %get-tuple-element.17.rank_ref, bf16[16,4,16,512]{3,2,1,0:T(8,128)(2,1)S(1)} %all_to_all.23.both_ref, ...), custom_call_target="tpu_custom_call" | custom-call | bytes 5242880 | tf_op jit(solution)/shard_map/update/pallas_call | solution.py:363
Async XLA Ops:
  1.9 50.9 %copy-start.3 = (s32[48]{0:T(128)S(1)}, s32[48]{0:T(128)}, u32[]{:S(2)}) copy-start(s32[48]{0:T(128)} %owners_ref) | copy-start | bytes 580
  48.3 6.0 %collective-permute-start = (bf16[256,512]{1,0:T(8,128)(2,1)S(1)}, bf16[256,512]{1,0:T(8,128)(2,1)S(1)}, u32[]{:S(2)}, u32[]{:S(2)}) collective-permute-start(bf16[256,512]{1,0:T(8,128)(2,1)S(1)} %bitcast.9), channel_id=1, source_target_pairs={{0,1},{1,0},{2,3},{3,2},{4,5},{5,4},{6,7},{7,6},{8,9},{9,8},{10,11... | collective-permute-start | bytes 786440 | tf_op jit(solution)/shard_map/gather_rows/ppermute | solution.py:321
  63.1 20.6 %copy-start.1 = (f32[48,16,512]{2,1,0:T(8,128)S(1)}, f32[48,16,512]{2,1,0:T(8,128)}, u32[]{:S(2)}) copy-start(f32[48,16,512]{2,1,0:T(8,128)} %weight_ref.1) | copy-start | bytes 4718596
  63.2 20.6 %copy-start = (bf16[1,48,16,512]{3,2,1,0:T(8,128)(2,1)S(1)}, bf16[1,48,16,512]{3,2,1,0:T(8,128)(2,1)}, u32[]{:S(2)}) copy-start(bf16[1,48,16,512]{3,2,1,0:T(8,128)(2,1)} %param.4) | copy-start | bytes 2359300
  63.2 20.6 %copy-start.2 = (f32[6,16,512]{2,1,0:T(8,128)S(1)}, f32[6,16,512]{2,1,0:T(8,128)}, u32[]{:S(2)}) copy-start(f32[6,16,512]{2,1,0:T(8,128)} %momentum_ref.1) | copy-start | bytes 589828

commit v8 on v7

--- a/solution.py
+++ b/solution.py
@@ -115,13 +115,13 @@
         copy.start()
     value = total_ref[0]
     for target in range(groups):
-        out_ref[target, per_group] = value
+        out_ref[target] = value
     for place in range(per_group):
         rank = place * groups + here_ref[0]
         owner = jnp.int32(-1)
         for group in range(groups):
             owner = owner + (first_ref[group] <= rank).astype(jnp.int32)
-        out_ref[owner, per_group] = total_ref[place]
+        out_ref[owner] = total_ref[place]
     for copy in copies:
         copy.wait()
 
@@ -184,8 +184,10 @@
 
 
 def spread_kernel(returned_ref, sums_ref, out_ref):
-    del sums_ref
-    for place in range(out_ref.shape[1] - 1):
+    per_group = out_ref.shape[1] - 1
+    for target in range(out_ref.shape[0]):
+        out_ref[target, per_group] = sums_ref[target]
+    for place in range(per_group):
         value = returned_ref[SEGMENT_ORDER.index(place)]
         for target in range(out_ref.shape[0]):
             out_ref[target, place] = value
@@ -250,15 +252,14 @@
         copy.wait()
 
 
-def call(kernel, out_shape, in_specs, scratch=(), flops=0, moved=0, out_specs=None, room=40.0, aliases={}):
+def call(kernel, out_shape, in_specs, scratch=(), flops=0, moved=0, out_specs=None):
     return pl.pallas_call(
         kernel,
         out_shape=out_shape,
         in_specs=in_specs,
         out_specs=jax.tree.map(lambda _: VMEM, out_shape) if out_specs is None else out_specs,
         scratch_shapes=list(scratch),
-        input_output_aliases=aliases,
-        compiler_params=pltpu.CompilerParams(vmem_limit_bytes=int((64 - room) * 1024 * 1024)),
+        compiler_params=pltpu.CompilerParams(vmem_limit_bytes=24 * 1024 * 1024),
         cost_estimate=pl.CostEstimate(flops=flops, bytes_accessed=moved, transcendentals=0),
     )
 
@@ -324,7 +325,7 @@
         sums, first, ranks = call(
             functools.partial(sums_kernel, groups),
             [
-                pltpu.VMEM((groups, per_group + 1, rows, order), jnp.bfloat16),
+                pltpu.VMEM((groups, rows, order), jnp.bfloat16),
                 pltpu.VMEM((groups,), jnp.int32),
                 pltpu.VMEM((blocks,), jnp.int32),
             ],
@@ -353,10 +354,9 @@
         )
         spread = call(
             spread_kernel,
-            bf16(sums.shape),
+            bf16((groups, per_group + 1, rows, order)),
             [VMEM, VMEM],
             moved=1 << 20,
-            aliases={1: 0},
         )(returned, sums)
         both = lax.all_to_all(spread, "rep", 0, 0, tiled=True)
     with jax.named_scope("update"):

time: 87.3 us -> 87.3 us (level)
  no operation moved by 1% of the time
where the time goes in v8:
time: 87.3 us; the launch traced here: 86.2 us
  blocking collectives  72.8 us (83%)
  Pallas kernels  8.16 us (9%)
  starting transfers between devices  4.46 us (5%)
    all_to_all x1, blocking collectives, on_device(): lax.all_to_all(send, 'fsdp', 0, 0, axis_index_groups=same_core, tiled=True)  31.2 us
    all_to_all x1, blocking collectives, on_device(): both = lax.all_to_all(spread, 'rep', 0, 0, tiled=True)  20.5 us
    all_to_all x1, blocking collectives, on_device(): lax.all_to_all(parts.reshape(groups, per_group, rows, order), 'rep', 0, 0...  15.1 us
    all_to_all x1, blocking collectives, on_device(): lax.all_to_all(kept.reshape(SEGMENT, rows, order), 'fsdp', 0, 0, axis_ind...  5.96 us
    ppermute x1, starting transfers between devices, on_device(): other = lax.ppermute(own, 'fsdp', [(i, i ^ 1) for i in range(members)])  4.46 us
    pallas_call x1, Pallas kernels, on_device(): call(newton_schulz_kernel, bf16((SEGMENT * rows, order)), [SMEM, VMEM, VM...  2.8 us
    pallas_call x1, Pallas kernels, on_device(): call(functools.partial(update_kernel, groups, 0.2 * math.sqrt(order)), [f...  2.4 us
  transfers between devices with their start and end apart: 1, of which 0 were waited for; matrix products, arithmetic and copies ran while one was open for 0% of the time, Pallas kernels for 2%

profile of v8, /device:TPU:1, one launch (start us, length us, event | category | flops | bytes accessed | tf_op | source)
XLA Modules:
  0.0 86.2 jit_solution(9499032605260929455)
XLA Ops:
  0.6 1.3 %fold_momentum.1 = bf16[48,16,512]{2,1,0:T(8,128)(2,1)S(1)} custom-call(s32[1]{0:T(128)} %bitcast.here_ref, s32[48]{0:T(128)} %owners_ref, bf16[48,16,512]{2,1,0:T(8,128)(2,1)} %bitcast.7, f32[6,16,512]{2,1,0:T(8,128)} %momentum_ref.1), custom_call_target="tpu_custom_call" | custom-call | bytes 2097152 | tf_op jit(solution)/shard_map/fold_momentum/pallas_call | solution.py:289
  1.9 0.0 copy-start.3
  1.9 15.1 %all_to_all.20.parts_ref = bf16[16,3,16,512]{3,2,1,0:T(8,128)(2,1)S(1)} all-to-all(bf16[16,3,16,512]{3,2,1,0:T(8,128)(2,1)S(1)} %bitcast.6), channel_id=1, replica_groups={{448,480,0,32,64,96,128,160,192,224,256,288,320,352,384,416},{449,481,1..., dimensions={0} | all-to-all | bytes 1572864 | tf_op jit(solution)/shard_map/reduce_over_rep/all_to_all | solution.py:305
  17.0 0.1 reduce_over_rep.1
  17.1 31.2 %all_to_all.21 = bf16[16,16,512]{2,1,0:T(8,128)(2,1)S(1)} all-to-all(bf16[16,16,512]{2,1,0:T(8,128)(2,1)S(1)} %get-tuple-element.12), channel_id=1, replica_groups={{22,20,18,16,14,12,10,8,6,4,2,0,30,28,26,24},{23,21,19,17,15,13,11,9,7,..., dimensions={0} | all-to-all | bytes 524288 | tf_op jit(solution)/shard_map/gather_rows/all_to_all | solution.py:320
  48.3 4.5 %collective-permute-start = (bf16[256,512]{1,0:T(8,128)(2,1)S(1)}, bf16[256,512]{1,0:T(8,128)(2,1)S(1)}, u32[]{:S(2)}, u32[]{:S(2)}) collective-permute-start(bf16[256,512]{1,0:T(8,128)(2,1)S(1)} %bitcast.9), channel_id=1, source_target_pairs={{0,1},{1,0},{2,3},{3,2},{4,5},{5,4},{6,7},{7,6},{8,9},{9,8},{10,11... | collective-permute-start | bytes 786440 | tf_op jit(solution)/shard_map/gather_rows/ppermute | solution.py:322
  52.8 0.0 copy-done.3
  52.8 1.5 %sums_to_owners.1 = (bf16[16,16,512]{2,1,0:T(8,128)(2,1)S(1)}, s32[16]{0:T(128)S(1)}, s32[48]{0:T(128)S(1)}) custom-call(s32[1]{0:T(128)} %bitcast.here_ref, s32[48]{0:T(128)S(1)} %copy-done.3, bf16[3,16,512]{2,1,0:T(8,128)(2,1)S(1)} %get-tuple-element.14.total_ref), custom_call_target="tpu_custom_call" | custom-call | bytes 1048576 | tf_op jit(solution)/shard_map/sums_to_owners/pallas_call | solution.py:325
  54.3 0.0 collective-permute-done.other_ref
  54.3 2.8 %orthogonalize.1 = bf16[64,512]{1,0:T(8,128)(2,1)S(1)} custom-call(s32[1]{0:T(128)} %bitcast.4.first_ref, bf16[256,512]{1,0:T(8,128)(2,1)S(1)} %bitcast.10, bf16[256,512]{1,0:T(8,128)(2,1)S(1)} %collective-permute-done.other_ref), custom_call_target="tpu_custom_call" | custom-call | flops 2013265920 | bytes 1048576 | tf_op jit(solution)/shard_map/orthogonalize/pallas_call | solution.py:343
  57.1 6.0 %all_to_all.22.returned_ref = bf16[4,16,512]{2,1,0:T(8,128)(2,1)S(1)} all-to-all(bf16[4,16,512]{2,1,0:T(8,128)(2,1)S(1)} %bitcast.11), channel_id=1, replica_groups={{4,2,6,0},{5,3,7,1},{12,10,14,8},{13,11,15,9},{20,18,22,16},{21,19,23,1..., dimensions={0} | all-to-all | bytes 131072 | tf_op jit(solution)/shard_map/return_rows/all_to_all | solution.py:352
  63.1 0.0 copy-start
  63.1 0.0 copy-start.1
  63.1 0.0 copy-start.2
  63.1 0.1 return_rows.1
  63.2 20.5 %all_to_all.23.both_ref = bf16[16,4,16,512]{3,2,1,0:T(8,128)(2,1)S(1)} all-to-all(bf16[16,4,16,512]{3,2,1,0:T(8,128)(2,1)S(1)} %return_rows.1), channel_id=1, replica_groups=mesh['rep'=16,'fsdp'=32] {'rep'}, dimensions={0} | all-to-all | bytes 2097152 | tf_op jit(solution)/shard_map/return_rows/all_to_all | solution.py:361
  83.7 0.0 copy-done
  83.7 0.0 copy-done.1
  83.7 0.0 copy-done.2
  83.7 2.4 %update.1 = (f32[48,16,512]{2,1,0:T(8,128)}, f32[48,16,512]{2,1,0:T(8,128)}, f32[6,16,512]{2,1,0:T(8,128)}) custom-call(s32[1]{0:T(128)} %bitcast.here_ref, s32[16]{0:T(128)S(1)} %get-tuple-element.15.first_ref, s32[48]{0:T(128)S(1)} %get-tuple-element.17.rank_ref, bf16[16,4,16,512]{3,2,1,0:T(8,128)(2,1)S(1)} %all_to_all.23.both_ref, ...), custom_call_target="tpu_custom_call" | custom-call | bytes 5242880 | tf_op jit(solution)/shard_map/update/pallas_call | solution.py:363
Async XLA Ops:
  1.9 50.9 %copy-start.3 = (s32[48]{0:T(128)S(1)}, s32[48]{0:T(128)}, u32[]{:S(2)}) copy-start(s32[48]{0:T(128)} %owners_ref) | copy-start | bytes 580
  48.3 6.0 %collective-permute-start = (bf16[256,512]{1,0:T(8,128)(2,1)S(1)}, bf16[256,512]{1,0:T(8,128)(2,1)S(1)}, u32[]{:S(2)}, u32[]{:S(2)}) collective-permute-start(bf16[256,512]{1,0:T(8,128)(2,1)S(1)} %bitcast.9), channel_id=1, source_target_pairs={{0,1},{1,0},{2,3},{3,2},{4,5},{5,4},{6,7},{7,6},{8,9},{9,8},{10,11... | collective-permute-start | bytes 786440 | tf_op jit(solution)/shard_map/gather_rows/ppermute | solution.py:322
  63.1 20.6 %copy-start = (bf16[1,48,16,512]{3,2,1,0:T(8,128)(2,1)S(1)}, bf16[1,48,16,512]{3,2,1,0:T(8,128)(2,1)}, u32[]{:S(2)}) copy-start(bf16[1,48,16,512]{3,2,1,0:T(8,128)(2,1)} %param.4) | copy-start | bytes 2359300
  63.1 20.6 %copy-start.1 = (f32[48,16,512]{2,1,0:T(8,128)S(1)}, f32[48,16,512]{2,1,0:T(8,128)}, u32[]{:S(2)}) copy-start(f32[48,16,512]{2,1,0:T(8,128)} %weight_ref.1) | copy-start | bytes 4718596
  63.1 20.6 %copy-start.2 = (f32[6,16,512]{2,1,0:T(8,128)S(1)}, f32[6,16,512]{2,1,0:T(8,128)}, u32[]{:S(2)}) copy-start(f32[6,16,512]{2,1,0:T(8,128)} %momentum_ref.1) | copy-start | bytes 589828

commit v9 on v8

--- a/solution.py
+++ b/solution.py
@@ -32,14 +32,14 @@
     return (part.astype(jnp.float32) + FOLD * momentum).astype(jnp.bfloat16)
 
 
-def count_slots(owners_ref, first_ref, rank_ref):
+def count_slots(owners_ref, first_ref, slot_ref):
     groups = first_ref.shape[0]
     for group in range(groups):
         first_ref[group] = 0
     for block in range(owners_ref.shape[0]):
         owner = owners_ref[block]
         slot = first_ref[owner]
-        rank_ref[block] = slot
+        slot_ref[block] = slot
         first_ref[owner] = slot + 1
     first = jnp.int32(0)
     for group in range(groups):
@@ -101,15 +101,13 @@
 
 
 def sums_kernel(
-    groups, here_ref, owners_ref, total_ref, out_ref, first_out_ref, rank_out_ref, first_ref, rank_ref, sems
+    groups, here_ref, owners_ref, total_ref, out_ref, first_out_ref, slot_out_ref, first_ref, slot_ref, sems
 ):
     per_group = total_ref.shape[0]
-    count_slots(owners_ref, first_ref, rank_ref)
-    for block in range(owners_ref.shape[0]):
-        rank_ref[block] = first_ref[owners_ref[block]] + rank_ref[block]
+    count_slots(owners_ref, first_ref, slot_ref)
     copies = [
         pltpu.make_async_copy(source, target, sems.at[index])
-        for index, (source, target) in enumerate([(first_ref, first_out_ref), (rank_ref, rank_out_ref)])
+        for index, (source, target) in enumerate([(first_ref, first_out_ref), (slot_ref, slot_out_ref)])
     ]
     for copy in copies:
         copy.start()
@@ -197,8 +195,9 @@
     groups,
     scale,
     here_ref,
+    owners_ref,
     first_ref,
-    rank_ref,
+    slot_ref,
     both_ref,
     weight_ref,
     part_ref,
@@ -225,7 +224,7 @@
     for index in range(PIECES):
         chunk = pl.ds(index * each, each)
         for block in range(index * each, (index + 1) * each):
-            group, place = split_rank(groups, rank_ref[block])
+            group, place = split_rank(groups, first_ref[owners_ref[block]] + slot_ref[block])
             step = both_ref[group, place].astype(jnp.float32) * scale
             step_ref[block] = step
             new_ref[block] = weight_ref[block] - LEARN_RATE * step
@@ -233,11 +232,11 @@
         leave(new_ref.at[chunk], new_hbm.at[chunk], sems.at[index, 1])
     here = here_ref[0]
     first = first_ref[here]
-    after = jnp.where(here == groups - 1, blocks, first_ref[jnp.minimum(here + 1, groups - 1)])
-    count = after - first
+    count = jnp.int32(0)
     for block in range(blocks):
-        slot = rank_ref[block] - first
-        owned_ref[jnp.where((slot >= 0) & (slot < count), slot, most)] = block
+        mine = owners_ref[block] == here
+        count = count + mine.astype(jnp.int32)
+        owned_ref[jnp.where(mine, slot_ref[block], most)] = block
     for slot in range(most):
         used = slot < count
         block = jnp.where(used, owned_ref[slot], 0)
@@ -322,7 +321,7 @@
         other = lax.ppermute(own, "fsdp", [(i, i ^ 1) for i in range(members)])
     with jax.named_scope("sums_to_owners"):
         late_owners, own = lax.optimization_barrier((owners, own))
-        sums, first, ranks = call(
+        sums, first, slots = call(
             functools.partial(sums_kernel, groups),
             [
                 pltpu.VMEM((groups, rows, order), jnp.bfloat16),
@@ -337,7 +336,7 @@
             ],
             moved=1 << 20,
         )(here, late_owners, total)
-        other, ranks = lax.optimization_barrier((other, ranks))
+        other, slots = lax.optimization_barrier((other, slots))
     with jax.named_scope("orthogonalize"):
         square = pltpu.VMEM((order, order), jnp.bfloat16)
         kept = call(
@@ -363,7 +362,7 @@
         return call(
             functools.partial(update_kernel, groups, 0.2 * math.sqrt(order)),
             [f32(weight.shape), f32(weight.shape), f32(momentum.shape)],
-            [SMEM, SMEM, SMEM, VMEM, VMEM, VMEM, VMEM],
+            [SMEM, SMEM, SMEM, SMEM, VMEM, VMEM, VMEM, VMEM],
             [
                 pltpu.SMEM((most + 1,), jnp.int32),
                 pltpu.VMEM(weight.shape, jnp.float32),
@@ -374,7 +373,7 @@
             ],
             moved=5 << 20,
             out_specs=[HBM, HBM, HBM],
-        )(here, first, ranks, both, weight, part, momentum)
+        )(here, late_owners, first, slots, both, weight, part, momentum)
 
 
 def solution(mesh):

time: 87.3 us -> 87.3 us (level)
  no operation moved by 1% of the time
where the time goes in v9:
time: 87.3 us; the launch traced here: 86.2 us
  blocking collectives  72.8 us (83%)
  Pallas kernels  8.1 us (9%)
  starting transfers between devices  4.46 us (5%)
    all_to_all x1, blocking collectives, on_device(): lax.all_to_all(send, 'fsdp', 0, 0, axis_index_groups=same_core, tiled=True)  31.2 us
    all_to_all x1, blocking collectives, on_device(): both = lax.all_to_all(spread, 'rep', 0, 0, tiled=True)  20.6 us
    all_to_all x1, blocking collectives, on_device(): lax.all_to_all(parts.reshape(groups, per_group, rows, order), 'rep', 0, 0...  15.1 us
    all_to_all x1, blocking collectives, on_device(): lax.all_to_all(kept.reshape(SEGMENT, rows, order), 'fsdp', 0, 0, axis_ind...  5.97 us
    ppermute x1, starting transfers between devices, on_device(): other = lax.ppermute(own, 'fsdp', [(i, i ^ 1) for i in range(members)])  4.46 us
    pallas_call x1, Pallas kernels, on_device(): call(newton_schulz_kernel, bf16((SEGMENT * rows, order)), [SMEM, VMEM, VM...  2.79 us
    pallas_call x1, Pallas kernels, on_device(): call(functools.partial(update_kernel, groups, 0.2 * math.sqrt(order)), [f...  2.42 us
  transfers between devices with their start and end apart: 1, of which 0 were waited for; matrix products, arithmetic and copies ran while one was open for 0% of the time, Pallas kernels for 2%

profile of v9, /device:TPU:1, one launch (start us, length us, event | category | flops | bytes accessed | tf_op | source)
XLA Modules:
  0.0 86.2 jit_solution(12265890508061977063)
XLA Ops:
  0.6 1.3 %fold_momentum.1 = bf16[48,16,512]{2,1,0:T(8,128)(2,1)S(1)} custom-call(s32[1]{0:T(128)} %bitcast.here_ref, s32[48]{0:T(128)} %owners_ref.1, bf16[48,16,512]{2,1,0:T(8,128)(2,1)} %bitcast.7, f32[6,16,512]{2,1,0:T(8,128)} %momentum_ref.1), custom_call_target="tpu_custom_call" | custom-call | bytes 2097152 | tf_op jit(solution)/shard_map/fold_momentum/pallas_call | solution.py:288
  1.9 0.0 copy-start.3
  1.9 15.1 %all_to_all.20.parts_ref = bf16[16,3,16,512]{3,2,1,0:T(8,128)(2,1)S(1)} all-to-all(bf16[16,3,16,512]{3,2,1,0:T(8,128)(2,1)S(1)} %bitcast.6), channel_id=1, replica_groups={{448,480,0,32,64,96,128,160,192,224,256,288,320,352,384,416},{449,481,1..., dimensions={0} | all-to-all | bytes 1572864 | tf_op jit(solution)/shard_map/reduce_over_rep/all_to_all | solution.py:304
  17.0 0.1 reduce_over_rep.1
  17.1 31.2 %all_to_all.21 = bf16[16,16,512]{2,1,0:T(8,128)(2,1)S(1)} all-to-all(bf16[16,16,512]{2,1,0:T(8,128)(2,1)S(1)} %get-tuple-element.12), channel_id=1, replica_groups={{22,20,18,16,14,12,10,8,6,4,2,0,30,28,26,24},{23,21,19,17,15,13,11,9,7,..., dimensions={0} | all-to-all | bytes 524288 | tf_op jit(solution)/shard_map/gather_rows/all_to_all | solution.py:319
  48.3 4.5 %collective-permute-start = (bf16[256,512]{1,0:T(8,128)(2,1)S(1)}, bf16[256,512]{1,0:T(8,128)(2,1)S(1)}, u32[]{:S(2)}, u32[]{:S(2)}) collective-permute-start(bf16[256,512]{1,0:T(8,128)(2,1)S(1)} %bitcast.9), channel_id=1, source_target_pairs={{0,1},{1,0},{2,3},{3,2},{4,5},{5,4},{6,7},{7,6},{8,9},{9,8},{10,11... | collective-permute-start | bytes 786440 | tf_op jit(solution)/shard_map/gather_rows/ppermute | solution.py:321
  52.8 0.0 copy-done.3
  52.8 1.4 %sums_to_owners.1 = (bf16[16,16,512]{2,1,0:T(8,128)(2,1)S(1)}, s32[16]{0:T(128)S(1)}, s32[48]{0:T(128)S(1)}) custom-call(s32[1]{0:T(128)} %bitcast.here_ref, s32[48]{0:T(128)S(1)} %copy-done.3, bf16[3,16,512]{2,1,0:T(8,128)(2,1)S(1)} %get-tuple-element.14.total_ref), custom_call_target="tpu_custom_call" | custom-call | bytes 1048576 | tf_op jit(solution)/shard_map/sums_to_owners/pallas_call | solution.py:324
  54.2 0.0 collective-permute-done.other_ref
  54.3 2.8 %orthogonalize.1 = bf16[64,512]{1,0:T(8,128)(2,1)S(1)} custom-call(s32[1]{0:T(128)} %bitcast.4.first_ref, bf16[256,512]{1,0:T(8,128)(2,1)S(1)} %bitcast.10, bf16[256,512]{1,0:T(8,128)(2,1)S(1)} %collective-permute-done.other_ref), custom_call_target="tpu_custom_call" | custom-call | flops 2013265920 | bytes 1048576 | tf_op jit(solution)/shard_map/orthogonalize/pallas_call | solution.py:342
  57.1 6.0 %all_to_all.22.returned_ref = bf16[4,16,512]{2,1,0:T(8,128)(2,1)S(1)} all-to-all(bf16[4,16,512]{2,1,0:T(8,128)(2,1)S(1)} %bitcast.11), channel_id=1, replica_groups={{4,2,6,0},{5,3,7,1},{12,10,14,8},{13,11,15,9},{20,18,22,16},{21,19,23,1..., dimensions={0} | all-to-all | bytes 131072 | tf_op jit(solution)/shard_map/return_rows/all_to_all | solution.py:351
  63.0 0.0 copy-start
  63.0 0.0 copy-start.1
  63.0 0.0 copy-start.2
  63.0 0.1 return_rows.1
  63.1 20.6 %all_to_all.23.both_ref = bf16[16,4,16,512]{3,2,1,0:T(8,128)(2,1)S(1)} all-to-all(bf16[16,4,16,512]{3,2,1,0:T(8,128)(2,1)S(1)} %return_rows.1), channel_id=1, replica_groups=mesh['rep'=16,'fsdp'=32] {'rep'}, dimensions={0} | all-to-all | bytes 2097152 | tf_op jit(solution)/shard_map/return_rows/all_to_all | solution.py:360
  83.7 0.0 copy-done
  83.7 0.0 copy-done.1
  83.7 0.0 copy-done.2
  83.7 2.4 %update.1 = (f32[48,16,512]{2,1,0:T(8,128)}, f32[48,16,512]{2,1,0:T(8,128)}, f32[6,16,512]{2,1,0:T(8,128)}) custom-call(s32[1]{0:T(128)} %bitcast.here_ref, s32[48]{0:T(128)S(1)} %copy-done.3, s32[16]{0:T(128)S(1)} %get-tuple-element.15.first_ref, s32[48]{0:T(128)S(1)} %get-tuple-element.17.slot_ref, bf16[16,4,16,512]{3,2,1,0:T(8,128)(2,1)S(1)} %all_to_all.23.both_ref, ...), custom_call_target="tpu_custom_call" | custom-call | bytes 5242880 | tf_op jit(solution)/shard_map/update/pallas_call | solution.py:362
Async XLA Ops:
  1.9 50.9 %copy-start.3 = (s32[48]{0:T(128)S(1)}, s32[48]{0:T(128)}, u32[]{:S(2)}) copy-start(s32[48]{0:T(128)} %owners_ref.1) | copy-start | bytes 580
  48.3 5.9 %collective-permute-start = (bf16[256,512]{1,0:T(8,128)(2,1)S(1)}, bf16[256,512]{1,0:T(8,128)(2,1)S(1)}, u32[]{:S(2)}, u32[]{:S(2)}) collective-permute-start(bf16[256,512]{1,0:T(8,128)(2,1)S(1)} %bitcast.9), channel_id=1, source_target_pairs={{0,1},{1,0},{2,3},{3,2},{4,5},{5,4},{6,7},{7,6},{8,9},{9,8},{10,11... | collective-permute-start | bytes 786440 | tf_op jit(solution)/shard_map/gather_rows/ppermute | solution.py:321
  63.0 20.7 %copy-start = (bf16[1,48,16,512]{3,2,1,0:T(8,128)(2,1)S(1)}, bf16[1,48,16,512]{3,2,1,0:T(8,128)(2,1)}, u32[]{:S(2)}) copy-start(bf16[1,48,16,512]{3,2,1,0:T(8,128)(2,1)} %param.4) | copy-start | bytes 2359300
  63.0 20.7 %copy-start.1 = (f32[48,16,512]{2,1,0:T(8,128)S(1)}, f32[48,16,512]{2,1,0:T(8,128)}, u32[]{:S(2)}) copy-start(f32[48,16,512]{2,1,0:T(8,128)} %weight_ref.1) | copy-start | bytes 4718596
  63.0 20.7 %copy-start.2 = (f32[6,16,512]{2,1,0:T(8,128)S(1)}, f32[6,16,512]{2,1,0:T(8,128)}, u32[]{:S(2)}) copy-start(f32[6,16,512]{2,1,0:T(8,128)} %momentum_ref.1) | copy-start | bytes 589828

commit v10 on v9

--- a/solution.py
+++ b/solution.py
@@ -18,7 +18,7 @@
 DIRECTION_SCALE = 1.0 + MOMENTUM_DECAY
 FOLD = MOMENTUM_DECAY * MOMENTUM_DECAY / DIRECTION_SCALE
 SEGMENT = 4
-PIECES = 6
+PIECES = 3
 FIRST_GROUP = 14
 TOP_SEGMENTS = 3
 SEGMENT_ORDER = (2, 1, 3, 0)
@@ -32,7 +32,7 @@
     return (part.astype(jnp.float32) + FOLD * momentum).astype(jnp.bfloat16)
 
 
-def count_slots(owners_ref, first_ref, slot_ref):
+def count_slots(owners_ref, first_ref, slot_ref, counted=lambda: None):
     groups = first_ref.shape[0]
     for group in range(groups):
         first_ref[group] = 0
@@ -41,6 +41,7 @@
         slot = first_ref[owner]
         slot_ref[block] = slot
         first_ref[owner] = slot + 1
+    counted()
     first = jnp.int32(0)
     for group in range(groups):
         after = first + first_ref[group]
@@ -104,13 +105,12 @@
     groups, here_ref, owners_ref, total_ref, out_ref, first_out_ref, slot_out_ref, first_ref, slot_ref, sems
 ):
     per_group = total_ref.shape[0]
-    count_slots(owners_ref, first_ref, slot_ref)
     copies = [
         pltpu.make_async_copy(source, target, sems.at[index])
         for index, (source, target) in enumerate([(first_ref, first_out_ref), (slot_ref, slot_out_ref)])
     ]
-    for copy in copies:
-        copy.start()
+    count_slots(owners_ref, first_ref, slot_ref, copies[1].start)
+    copies[0].start()
     value = total_ref[0]
     for target in range(groups):
         out_ref[target] = value

time: 87.3 us -> 87.3 us (level)
  no operation moved by 1% of the time
where the time goes in v10:
time: 87.3 us; the launch traced here: 86.1 us
  blocking collectives  72.8 us (83%)
  Pallas kernels  8.11 us (9%)
  starting transfers between devices  4.46 us (5%)
    all_to_all x1, blocking collectives, on_device(): lax.all_to_all(send, 'fsdp', 0, 0, axis_index_groups=same_core, tiled=True)  31.2 us
    all_to_all x1, blocking collectives, on_device(): both = lax.all_to_all(spread, 'rep', 0, 0, tiled=True)  20.6 us
    all_to_all x1, blocking collectives, on_device(): lax.all_to_all(parts.reshape(groups, per_group, rows, order), 'rep', 0, 0...  15.1 us
    all_to_all x1, blocking collectives, on_device(): lax.all_to_all(kept.reshape(SEGMENT, rows, order), 'fsdp', 0, 0, axis_ind...  5.97 us
    ppermute x1, starting transfers between devices, on_device(): other = lax.ppermute(own, 'fsdp', [(i, i ^ 1) for i in range(members)])  4.46 us
    pallas_call x1, Pallas kernels, on_device(): call(newton_schulz_kernel, bf16((SEGMENT * rows, order)), [SMEM, VMEM, VM...  2.8 us
    pallas_call x1, Pallas kernels, on_device(): call(functools.partial(update_kernel, groups, 0.2 * math.sqrt(order)), [f...  2.42 us
  transfers between devices with their start and end apart: 1, of which 0 were waited for; matrix products, arithmetic and copies ran while one was open for 0% of the time, Pallas kernels for 2%

profile of v10, /device:TPU:1, one launch (start us, length us, event | category | flops | bytes accessed | tf_op | source)
XLA Modules:
  0.0 86.1 jit_solution(4661514334196787141)
XLA Ops:
  0.6 1.3 %fold_momentum.1 = bf16[48,16,512]{2,1,0:T(8,128)(2,1)S(1)} custom-call(s32[1]{0:T(128)} %bitcast.here_ref, s32[48]{0:T(128)} %owners_ref.1, bf16[48,16,512]{2,1,0:T(8,128)(2,1)} %bitcast.7, f32[6,16,512]{2,1,0:T(8,128)} %momentum_ref.1), custom_call_target="tpu_custom_call" | custom-call | bytes 2097152 | tf_op jit(solution)/shard_map/fold_momentum/pallas_call | solution.py:288
  1.9 0.0 copy-start.3
  1.9 15.1 %all_to_all.20.parts_ref = bf16[16,3,16,512]{3,2,1,0:T(8,128)(2,1)S(1)} all-to-all(bf16[16,3,16,512]{3,2,1,0:T(8,128)(2,1)S(1)} %bitcast.6), channel_id=1, replica_groups={{448,480,0,32,64,96,128,160,192,224,256,288,320,352,384,416},{449,481,1..., dimensions={0} | all-to-all | bytes 1572864 | tf_op jit(solution)/shard_map/reduce_over_rep/all_to_all | solution.py:304
  17.0 0.1 reduce_over_rep.1
  17.1 31.2 %all_to_all.21 = bf16[16,16,512]{2,1,0:T(8,128)(2,1)S(1)} all-to-all(bf16[16,16,512]{2,1,0:T(8,128)(2,1)S(1)} %get-tuple-element.12), channel_id=1, replica_groups={{22,20,18,16,14,12,10,8,6,4,2,0,30,28,26,24},{23,21,19,17,15,13,11,9,7,..., dimensions={0} | all-to-all | bytes 524288 | tf_op jit(solution)/shard_map/gather_rows/all_to_all | solution.py:319
  48.3 4.5 %collective-permute-start = (bf16[256,512]{1,0:T(8,128)(2,1)S(1)}, bf16[256,512]{1,0:T(8,128)(2,1)S(1)}, u32[]{:S(2)}, u32[]{:S(2)}) collective-permute-start(bf16[256,512]{1,0:T(8,128)(2,1)S(1)} %bitcast.9), channel_id=1, source_target_pairs={{0,1},{1,0},{2,3},{3,2},{4,5},{5,4},{6,7},{7,6},{8,9},{9,8},{10,11... | collective-permute-start | bytes 786440 | tf_op jit(solution)/shard_map/gather_rows/ppermute | solution.py:321
  52.8 0.0 copy-done.3
  52.8 1.4 %sums_to_owners.1 = (bf16[16,16,512]{2,1,0:T(8,128)(2,1)S(1)}, s32[16]{0:T(128)S(1)}, s32[48]{0:T(128)S(1)}) custom-call(s32[1]{0:T(128)} %bitcast.here_ref, s32[48]{0:T(128)S(1)} %copy-done.3, bf16[3,16,512]{2,1,0:T(8,128)(2,1)S(1)} %get-tuple-element.14.total_ref), custom_call_target="tpu_custom_call" | custom-call | bytes 1048576 | tf_op jit(solution)/shard_map/sums_to_owners/pallas_call | solution.py:324
  54.3 0.0 collective-permute-done.other_ref
  54.3 2.8 %orthogonalize.1 = bf16[64,512]{1,0:T(8,128)(2,1)S(1)} custom-call(s32[1]{0:T(128)} %bitcast.4.first_ref, bf16[256,512]{1,0:T(8,128)(2,1)S(1)} %bitcast.10, bf16[256,512]{1,0:T(8,128)(2,1)S(1)} %collective-permute-done.other_ref), custom_call_target="tpu_custom_call" | custom-call | flops 2013265920 | bytes 1048576 | tf_op jit(solution)/shard_map/orthogonalize/pallas_call | solution.py:342
  57.1 6.0 %all_to_all.22.returned_ref = bf16[4,16,512]{2,1,0:T(8,128)(2,1)S(1)} all-to-all(bf16[4,16,512]{2,1,0:T(8,128)(2,1)S(1)} %bitcast.11), channel_id=1, replica_groups={{4,2,6,0},{5,3,7,1},{12,10,14,8},{13,11,15,9},{20,18,22,16},{21,19,23,1..., dimensions={0} | all-to-all | bytes 131072 | tf_op jit(solution)/shard_map/return_rows/all_to_all | solution.py:351
  63.0 0.0 copy-start
  63.0 0.0 copy-start.1
  63.0 0.0 copy-start.2
  63.0 0.1 return_rows.1
  63.1 20.6 %all_to_all.23.both_ref = bf16[16,4,16,512]{3,2,1,0:T(8,128)(2,1)S(1)} all-to-all(bf16[16,4,16,512]{3,2,1,0:T(8,128)(2,1)S(1)} %return_rows.1), channel_id=1, replica_groups=mesh['rep'=16,'fsdp'=32] {'rep'}, dimensions={0} | all-to-all | bytes 2097152 | tf_op jit(solution)/shard_map/return_rows/all_to_all | solution.py:360
  83.7 0.0 copy-done
  83.7 0.0 copy-done.1
  83.7 0.0 copy-done.2
  83.7 2.4 %update.1 = (f32[48,16,512]{2,1,0:T(8,128)}, f32[48,16,512]{2,1,0:T(8,128)}, f32[6,16,512]{2,1,0:T(8,128)}) custom-call(s32[1]{0:T(128)} %bitcast.here_ref, s32[48]{0:T(128)S(1)} %copy-done.3, s32[16]{0:T(128)S(1)} %get-tuple-element.15.first_ref, s32[48]{0:T(128)S(1)} %get-tuple-element.17.slot_ref, bf16[16,4,16,512]{3,2,1,0:T(8,128)(2,1)S(1)} %all_to_all.23.both_ref, ...), custom_call_target="tpu_custom_call" | custom-call | bytes 5242880 | tf_op jit(solution)/shard_map/update/pallas_call | solution.py:362
Async XLA Ops:
  1.9 50.9 %copy-start.3 = (s32[48]{0:T(128)S(1)}, s32[48]{0:T(128)}, u32[]{:S(2)}) copy-start(s32[48]{0:T(128)} %owners_ref.1) | copy-start | bytes 580
  48.3 5.9 %collective-permute-start = (bf16[256,512]{1,0:T(8,128)(2,1)S(1)}, bf16[256,512]{1,0:T(8,128)(2,1)S(1)}, u32[]{:S(2)}, u32[]{:S(2)}) collective-permute-start(bf16[256,512]{1,0:T(8,128)(2,1)S(1)} %bitcast.9), channel_id=1, source_target_pairs={{0,1},{1,0},{2,3},{3,2},{4,5},{5,4},{6,7},{7,6},{8,9},{9,8},{10,11... | collective-permute-start | bytes 786440 | tf_op jit(solution)/shard_map/gather_rows/ppermute | solution.py:321
  63.0 20.7 %copy-start = (bf16[1,48,16,512]{3,2,1,0:T(8,128)(2,1)S(1)}, bf16[1,48,16,512]{3,2,1,0:T(8,128)(2,1)}, u32[]{:S(2)}) copy-start(bf16[1,48,16,512]{3,2,1,0:T(8,128)(2,1)} %param.4) | copy-start | bytes 2359300
  63.0 20.7 %copy-start.1 = (f32[48,16,512]{2,1,0:T(8,128)S(1)}, f32[48,16,512]{2,1,0:T(8,128)}, u32[]{:S(2)}) copy-start(f32[48,16,512]{2,1,0:T(8,128)} %weight_ref.1) | copy-start | bytes 4718596
  63.0 20.7 %copy-start.2 = (f32[6,16,512]{2,1,0:T(8,128)S(1)}, f32[6,16,512]{2,1,0:T(8,128)}, u32[]{:S(2)}) copy-start(f32[6,16,512]{2,1,0:T(8,128)} %momentum_ref.1) | copy-start | bytes 589828
